TPU v7x, 512 devices: a whole 4x8x8 slice. The times are simulated.
512 devices in a mesh: dp: 16 (over y, core), group: 32 (over x, z).
Axes of the slice: x: 4, y: 8, z: 8, core: 2. Of those that a mesh axis runs over, the one named last changes fastest.
Arguments:
- partial_stats: bfloat16 [16, 16, 1024, 1024], P('dp', None, 'group'), as said below
- old_basis: bfloat16 [16, 2, 1024, 1024], P('dp', None, 'group'), as said below
- exp_avg: float32 [16, 2, 1024, 4096], P('dp', None, None, 'group'), may hold values from -6 to 6
- slot_block: int32 [16, 2], replicated, may hold values from -1 to 15, as said below
Outputs:
- exp_avg_new: float32 [16, 2, 1024, 4096], P('dp', None, None, 'group')
Inputs may be any that keep to these rules, and one draw needn't show every extreme that they name: `slot_block`: row d lists the blocks refreshed by data-parallel row d, used slots first and -1 in the rest; every block 0 to 15 stands in exactly one slot. Some row uses all 2 slots and some row none. `partial_stats`: each replica's share is symmetric; the sum over replicas of one block is symmetric positive definite. `old_basis`: each matrix is well conditioned.
All inputs are finite; a program needn't handle non-finite values.
Results may differ from a plain program's by a relative error of at most 0.015.
Values may be sent and summed in bfloat16 or wider, within the bound.
No kernel may reach another device: no remote copies, remote signals or barrier semaphores. Data moves between devices by JAX's collectives and lax.ppermute only.
A program may use at most 64 MiB of HBM per device.

v0:
```python
import jax
import jax.numpy as jnp
from jax import lax
from jax.sharding import PartitionSpec as P


def on_device(partial_stats, old_basis, exp_avg, slot_block):
    slab_rows = partial_stats.shape[2]
    order_size = partial_stats.shape[3]
    group_offset = lax.axis_index("group") * slab_rows
    own_slots = lax.dynamic_index_in_dim(slot_block, lax.axis_index("dp"), 0, keepdims=False)
    row_iota = lax.broadcasted_iota(jnp.int32, (slab_rows, order_size), 0)
    column_iota = lax.broadcasted_iota(jnp.int32, (slab_rows, order_size), 1)
    identity_slab = (row_iota + group_offset == column_iota).astype(jnp.float32)
    local_stats = partial_stats[0]
    totals = lax.psum(local_stats.astype(jnp.float32).astype(jnp.bfloat16), "dp").astype(
        jnp.float32
    )
    summed_slabs = jnp.take(totals, jnp.maximum(own_slots, 0), axis=0)

    def refresh_slot(operands):
        block_id, summed, previous_raw, moment = operands
        slot_live = block_id >= 0
        factor_low = jnp.where(slot_live, summed, identity_slab).astype(jnp.bfloat16)
        previous = jnp.where(slot_live, previous_raw, identity_slab.astype(jnp.bfloat16))
        previous_full = lax.all_gather(previous, "group", axis=0, tiled=True)
        projected = jnp.dot(factor_low, previous_full, preferred_element_type=jnp.float32).astype(
            jnp.bfloat16
        )
        back_moment = jnp.dot(
            previous_full.astype(jnp.float32), moment, precision=lax.Precision.HIGHEST
        )
        projected_full = lax.all_gather(projected, "group", axis=0, tiled=True)
        gram_total = jnp.dot(projected_full.T, projected_full, preferred_element_type=jnp.float32)
        lower_factor = jnp.linalg.cholesky(gram_total)
        solved = jax.scipy.linalg.solve_triangular(
            lower_factor, projected.astype(jnp.float32).T, lower=True
        )
        new_basis = solved.T.astype(jnp.bfloat16)
        basis_full = lax.all_gather(new_basis, "group", axis=0, tiled=True)
        rotated = jnp.dot(
            basis_full.astype(jnp.float32).T, back_moment, precision=lax.Precision.HIGHEST
        )
        return jnp.where(slot_live, rotated, jnp.zeros_like(rotated))

    rotated_slots = lax.map(refresh_slot, (own_slots, summed_slabs, old_basis[0], exp_avg[0]))
    return rotated_slots[None]


def solution(mesh):
    return jax.shard_map(
        on_device,
        mesh=mesh,
        in_specs=(
            P("dp", None, "group", None),
            P("dp", None, "group", None),
            P("dp", None, None, "group"),
            P(),
        ),
        out_specs=P("dp", None, None, "group"),
        check_vma=False,
    )
```

profile of v0, /device:TPU:6, one launch (start us, length us, event | category | flops | bytes accessed | tf_op | source)
XLA Modules:
  0.0 1336.1 jit_solution(14292603068170671841)
XLA Ops:
  8.2 122.9 %all-reduce.3.cloned.1.call-done = bf16[16,32,1024]{2,1,0:T(8,128)(2,1)} async-done(((bf16[16,32,1024]{2,1,0:T(8,128)(2,1)}), bf16[16,32,1024]{2,1,0:T(8,128)(2,1)}) %all-reduce.3.cloned.1.call-update) | async-done | bytes 1048592 | tf_op jit(solution)/shard_map/psum | solution.py:16
  133.0 1196.0 %while.18 = (s32[]{:T(128)}, f32[2,1024,128]{2,1,0:T(8,128)}, s32[2]{0:T(128)S(1)}, bf16[2,32,1024]{2,1,0:T(8,128)(2,1)S(1)}, bf16[2,32,1024]{2,1,0:T(8,128)(2,1...) while((s32[]{:T(128)}, f32[2,1024,128]{2,1,0:T(8,128)}, ...), condition=%wide.region_18.19_spmd.clone.clone, body=%wide.region_1.18_spmd.clone.clone.sunk | while | flops 8488825344 | bytes 114984728 | solution.py:46
  136.3 85.2 %all-gather.4.cloned.1.call-done = bf16[1024,1024]{1,0:T(8,128)(2,1)} async-done(((bf16[32,1024]{1,0:T(8,128)(2,1)}), bf16[1024,1024]{1,0:T(8,128)(2,1)}) %all-gather.4.cloned.1.call-update) | async-done | bytes 2097168 | tf_op jit(solution)/shard_map/while/body/eval_jaxpr/all_gather | solution.py:26
  224.3 81.7 %all-gather.6.cloned.1.call-done = bf16[1024,1024]{1,0:T(8,128)(2,1)} async-done(((bf16[32,1024]{1,0:T(8,128)(2,1)}), bf16[1024,1024]{1,0:T(8,128)(2,1)}) %all-gather.6.cloned.1.call-update) | async-done | bytes 2097168 | tf_op jit(solution)/shard_map/while/body/eval_jaxpr/all_gather | solution.py:33
  324.5 11.7 cholesky.1214
  336.3 9.8 custom-call.120
  352.5 12.3 cholesky.1217
  378.7 11.7 cholesky.1219
  405.0 11.8 cholesky.1221
  431.4 11.7 cholesky.1223
  444.5 10.0 custom-call.124
  457.8 11.7 cholesky.1225
  483.6 12.1 cholesky.1227
  509.3 11.7 cholesky.1228
  532.8 22.9 %while.19 = (s32[]{:T(128)}, f32[1024,1024]{1,0:T(8,128)}, s32[8,2]{0,1:T(2,128)S(1)}, f32[8,128,128]{2,1,0:T(8,128)S(1)}, s32[]{:T(128)}) while((s32[]{:T(128)}, f32[1024,1024]{1,0:T(8,128)}, s32[8,2]{0,1:T(2,128)S(1)}, f32[8,128,128]{2,1,0:T(8,128)S(1)}, s32[]{:T(128)}) %tuple.132), condition=%wide.while_cond, body=%wide.while_body.sunk | while | flops 2 | bytes 131189 | solution.py:36
  555.7 78.8 %custom-call.128 = f32[8,128,128]{1,2,0:T(8,128)S(1)} custom-call(f32[8,128,128]{2,1,0:T(8,128)S(1)} %get-tuple-element.372), custom_call_target="InvertDiagBlocksLowerTriangular" | custom-call | tf_op jit(solution)/shard_map/while/body/eval_jaxpr/jit(_solve_triangular)/triangular_solve | solution.py:36
  649.5 78.1 %all-gather.8.cloned.1.call-done = bf16[1024,1024]{1,0:T(8,128)(2,1)} async-done(((bf16[32,1024]{1,0:T(8,128)(2,1)}), bf16[1024,1024]{1,0:T(8,128)(2,1)}) %all-gather.8.cloned.1.call-update) | async-done | bytes 2097168 | tf_op jit(solution)/shard_map/while/body/eval_jaxpr/all_gather | solution.py:40
  735.5 82.0 %all-gather.4.cloned.1.call-done = bf16[1024,1024]{1,0:T(8,128)(2,1)} async-done(((bf16[32,1024]{1,0:T(8,128)(2,1)}), bf16[1024,1024]{1,0:T(8,128)(2,1)}) %all-gather.4.cloned.1.call-update) | async-done | bytes 2097168 | tf_op jit(solution)/shard_map/while/body/eval_jaxpr/all_gather | solution.py:26
  820.3 81.5 %all-gather.6.cloned.1.call-done = bf16[1024,1024]{1,0:T(8,128)(2,1)} async-done(((bf16[32,1024]{1,0:T(8,128)(2,1)}), bf16[1024,1024]{1,0:T(8,128)(2,1)}) %all-gather.6.cloned.1.call-update) | async-done | bytes 2097168 | tf_op jit(solution)/shard_map/while/body/eval_jaxpr/all_gather | solution.py:33
  920.3 11.7 cholesky.1214
  932.1 9.8 custom-call.120
  948.3 12.2 cholesky.1217
  974.3 11.7 cholesky.1219
  1000.6 11.8 cholesky.1221
  1027.0 11.7 cholesky.1223
  1040.1 10.0 custom-call.124
  1053.4 11.7 cholesky.1225
  1079.2 12.1 cholesky.1227
  1105.0 11.7 cholesky.1228
  1128.4 22.9 %while.19 = (s32[]{:T(128)}, f32[1024,1024]{1,0:T(8,128)}, s32[8,2]{0,1:T(2,128)S(1)}, f32[8,128,128]{2,1,0:T(8,128)S(1)}, s32[]{:T(128)}) while((s32[]{:T(128)}, f32[1024,1024]{1,0:T(8,128)}, s32[8,2]{0,1:T(2,128)S(1)}, f32[8,128,128]{2,1,0:T(8,128)S(1)}, s32[]{:T(128)}) %tuple.132), condition=%wide.while_cond, body=%wide.while_body.sunk | while | flops 2 | bytes 131189 | solution.py:36
  1151.3 78.8 %custom-call.128 = f32[8,128,128]{1,2,0:T(8,128)S(1)} custom-call(f32[8,128,128]{2,1,0:T(8,128)S(1)} %get-tuple-element.372), custom_call_target="InvertDiagBlocksLowerTriangular" | custom-call | tf_op jit(solution)/shard_map/while/body/eval_jaxpr/jit(_solve_triangular)/triangular_solve | solution.py:36
  1245.1 78.1 %all-gather.8.cloned.1.call-done = bf16[1024,1024]{1,0:T(8,128)(2,1)} async-done(((bf16[32,1024]{1,0:T(8,128)(2,1)}), bf16[1024,1024]{1,0:T(8,128)(2,1)}) %all-gather.8.cloned.1.call-update) | async-done | bytes 2097168 | tf_op jit(solution)/shard_map/while/body/eval_jaxpr/all_gather | solution.py:40
  (233 shorter events, 312.4 us)
Async XLA Ops:
  6.5 124.5 %all-reduce.3.cloned.1.call-start = ((), (), s32[]{:S(2)}) async-start(), calls=%async_computation | async-start | bytes 2097152 | tf_op jit(solution)/shard_map/psum | solution.py:16
  133.2 88.2 %all-gather.4.cloned.1.call-start = ((), (), s32[]{:S(2)}) async-start(), calls=%async_computation.1 | async-start | bytes 2162688 | tf_op jit(solution)/shard_map/while/body/eval_jaxpr/all_gather | solution.py:26
  136.2 169.7 %all-gather.6.cloned.1.call-start = ((), (), s32[]{:S(2)}) async-start(), calls=%async_computation.2 | async-start | bytes 2162688 | tf_op jit(solution)/shard_map/while/body/eval_jaxpr/all_gather | solution.py:33
  224.2 503.4 %all-gather.8.cloned.1.call-start = ((), (), s32[]{:S(2)}) async-start(), calls=%async_computation.3 | async-start | bytes 2162688 | tf_op jit(solution)/shard_map/while/body/eval_jaxpr/all_gather | solution.py:40
  322.6 1.9 copy-start
  532.8 113.8 %copy-start.1 = (bf16[1024,1024]{1,0:T(8,128)(2,1)S(1)}, bf16[1024,1024]{1,0:T(8,128)(2,1)}, u32[]{:S(2)}) copy-start(bf16[1024,1024]{1,0:T(8,128)(2,1)} %all-gather.4.cloned.1.call-done) | copy-start | bytes 6291460 | tf_op jit(solution)/shard_map/while
  646.0 0.6 copy-start.2
  732.5 85.0 %all-gather.4.cloned.1.call-start = ((), (), s32[]{:S(2)}) async-start(), calls=%async_computation.1 | async-start | bytes 2162688 | tf_op jit(solution)/shard_map/while/body/eval_jaxpr/all_gather | solution.py:26
  735.5 166.4 %all-gather.6.cloned.1.call-start = ((), (), s32[]{:S(2)}) async-start(), calls=%async_computation.2 | async-start | bytes 2162688 | tf_op jit(solution)/shard_map/while/body/eval_jaxpr/all_gather | solution.py:33
  820.2 503.0 %all-gather.8.cloned.1.call-start = ((), (), s32[]{:S(2)}) async-start(), calls=%async_computation.3 | async-start | bytes 2162688 | tf_op jit(solution)/shard_map/while/body/eval_jaxpr/all_gather | solution.py:40
  918.4 1.9 copy-start
  1128.4 113.8 %copy-start.1 = (bf16[1024,1024]{1,0:T(8,128)(2,1)S(1)}, bf16[1024,1024]{1,0:T(8,128)(2,1)}, u32[]{:S(2)}) copy-start(bf16[1024,1024]{1,0:T(8,128)(2,1)} %all-gather.4.cloned.1.call-done) | copy-start | bytes 6291460 | tf_op jit(solution)/shard_map/while
  1241.6 0.6 copy-start.2
Sparse Core Ops, SparseCore 0:
  9.7 121.3 all-reduce.2
  137.7 83.6 all-gather.3
  225.1 80.7 all-gather.5
  646.8 80.7 all-gather.7
  736.7 80.7 all-gather.3
  821.0 80.7 all-gather.5
  1242.4 80.7 all-gather.7
where the time goes:
time: 1340 us
  waiting for transfers between devices  610 us (46%)
  other arithmetic  526 us (39%)
  matrix products  102 us (8%)
  local copies, waits for them, and re-layouts  70.1 us (5%)
  loops' own time  14 us (1%)
  between operations  13.7 us (1%)
    another operation x60, other arithmetic, refresh_slot(): lower_factor = jnp.linalg.cholesky(gram_total)  345 us
    all_gather x2, waiting for transfers between devices, refresh_slot(): previous_full = lax.all_gather(previous, 'group', axis=0, tiled=True)  167 us
    another operation x6, other arithmetic, refresh_slot(): jax.scipy.linalg.solve_triangular(lower_factor, projected.astype(jnp.floa...  167 us
    all_gather x2, waiting for transfers between devices, refresh_slot(): projected_full = lax.all_gather(projected, 'group', axis=0, tiled=True)  163 us
    all_gather x2, waiting for transfers between devices, refresh_slot(): basis_full = lax.all_gather(new_basis, 'group', axis=0, tiled=True)  156 us
    psum x1, waiting for transfers between devices, on_device(): lax.psum(local_stats.astype(jnp.float32).astype(jnp.bfloat16), 'dp')  123 us
    another operation x28, matrix products, refresh_slot(): lower_factor = jnp.linalg.cholesky(gram_total)  46.1 us
    another operation x48, local copies, waits for them, and re-layouts  45.4 us
  transfers between devices with their start and end apart: 7, of which 7 were waited for; matrix products, arithmetic and copies ran while one was open for 0% of the time, Pallas kernels for 0%

commit v1 on v0

v1 whole, which is shorter than its diff:
```python
import functools

import jax
import jax.numpy as jnp
from jax import lax
from jax.experimental import pallas as pl
from jax.experimental.pallas import tpu as pltpu
from jax.sharding import PartitionSpec as P

BF16, F32 = jnp.bfloat16, jnp.float32
VMEM_BYTES = 48 * 1024 * 1024
TILE = 128
SUB = 8
X_CHIPS, Z_CHIPS = 4, 8


def high_low(value):
    high = value.astype(BF16)
    return high, (value - high.astype(F32)).astype(BF16)


def from_neighbour(value, dx, dz):
    pairs = []
    for x in range(X_CHIPS):
        for z in range(Z_CHIPS):
            source = (x + dx) % X_CHIPS * Z_CHIPS + (z + dz) % Z_CHIPS
            pairs.append((source, x * Z_CHIPS + z))
    return lax.ppermute(value, "group", pairs)


def gather_rows(slab):
    pieces = [slab] + [None] * (Z_CHIPS - 1)
    for dz in (1, -1, 2, -2):
        pieces[dz % Z_CHIPS] = from_neighbour(slab, 0, dz)
    pieces[3] = from_neighbour(pieces[2], 0, 1)
    pieces[5] = from_neighbour(pieces[6], 0, -1)
    far_first = from_neighbour(pieces[2][:1], 0, 2)
    far_second = from_neighbour(pieces[6][1:], 0, -2)
    pieces[4] = jnp.concatenate([far_first, far_second], axis=0)
    own = jnp.stack(pieces, axis=1).reshape(2, Z_CHIPS * slab.shape[1], slab.shape[2])
    after = from_neighbour(own, 1, 0)
    before = from_neighbour(own, -1, 0)
    across_first = from_neighbour(after[0], 1, 0)
    across_second = from_neighbour(before[1], -1, 0)
    return own, after, across_first, across_second, before


def quarter(refs, slot, distance):
    own, after, across_first, across_second, before = refs
    if distance == 2:
        return (across_first, across_second)[slot][...]
    return (own, after, None, before)[distance][slot]


def back_kernel(*refs):
    rows, moment, out = refs[:5], refs[5], refs[6]
    for slot in range(2):
        high, low = high_low(moment[slot])
        both = jnp.concatenate([high, low], axis=1)
        for distance in range(X_CHIPS):
            block = quarter(rows, slot, distance)
            size = block.shape[0]
            product = jnp.dot(block, both, preferred_element_type=F32)
            width = high.shape[1]
            high_back, low_back = high_low(product[:, :width] + product[:, width:])
            out[slot, distance * size : (distance + 1) * size, :] = jnp.concatenate([high_back, low_back], axis=1)


def project_kernel(place, factor, *refs):
    rows, out = refs[:5], refs[5]
    x, z = place[0], place[1]
    for slot in range(2):
        total = jnp.zeros(out.shape[1:], F32)
        for distance in range(X_CHIPS):
            block = quarter(rows, slot, distance)
            size = block.shape[0]
            at = lax.rem(x + distance, X_CHIPS) * size
            part = factor[slot, :, pl.ds(pl.multiple_of(at, size), size)].astype(F32)
            step = size // Z_CHIPS
            part = pltpu.roll(part, lax.rem((Z_CHIPS - z) * step, size), 1)
            total += jnp.dot(part.astype(BF16), block, preferred_element_type=F32)
        out[slot] = total.astype(BF16)


def row_of(value, at):
    return jnp.broadcast_to(value[at : at + 1, :], value.shape)


def lane_of(value, at):
    return jnp.broadcast_to(value[:, at : at + 1], value.shape)


def inverse_factors(work, inverse):
    lane = lax.broadcasted_iota(jnp.int32, (SUB, TILE), 1)
    upper_half = lax.broadcasted_iota(jnp.int32, (SUB, TILE), 0) < SUB // 2
    n_sub = TILE // SUB
    tiles = [[work[slot, SUB * i : SUB * (i + 1), :] for i in range(n_sub)] for slot in range(2)]
    for s in range(n_sub):
        first = SUB * s
        inside = (lane >= first) & (lane < first + SUB)
        rows = [jnp.where(upper_half, row_of(tiles[0][s], r), row_of(tiles[1][s], r)) for r in range(SUB)]
        entry = [[lane_of(rows[r], first + c) for c in range(r + 1)] for r in range(SUB)]
        rows = [jnp.where(inside, jnp.where(lane == first + r, 1.0, 0.0), rows[r]) for r in range(SUB)]
        ratio = [[None] * SUB for _ in range(SUB)]
        inverse_pivot = [None] * SUB
        for k in range(SUB):
            inverse_pivot[k] = 1.0 / entry[k][k]
            for r in range(k + 1, SUB):
                ratio[r][k] = entry[r][k] * inverse_pivot[k]
            for r in range(k + 1, SUB):
                for c in range(k + 1, r + 1):
                    entry[r][c] = entry[r][c] - ratio[r][k] * entry[c][k]
                rows[r] = rows[r] - ratio[r][k] * rows[k]
        solved = [None] * SUB
        for k in reversed(range(SUB)):
            value = rows[k] * inverse_pivot[k]
            for r in reversed(range(k + 1, SUB)):
                value = value - ratio[r][k] * solved[r]
            solved[k] = value
        for k in range(SUB):
            scaled = jnp.where(lane < first + SUB, rows[k] * lax.rsqrt(entry[k][k]), 0.0)
            for slot in range(2):
                at = slot * (SUB // 2)
                inverse[slot, first + k : first + k + 1, :] = scaled[at : at + 1, :]
        if s + 1 == n_sub:
            break
        for slot in range(2):
            spread = [row_of(solved[k], slot * (SUB // 2)) for k in range(SUB)]
            for i in range(s + 1, n_sub):
                old = tiles[slot][i]
                terms = [lane_of(old, first + c) * spread[c] for c in range(SUB)]
                while len(terms) > 1:
                    terms = [a + b for a, b in zip(terms[::2], terms[1::2])]
                tiles[slot][i] = jnp.where(inside, 0.0, old) - terms[0]


def eliminate_kernel(live, *refs):
    rows, back, out = refs[:5], refs[5], refs[6]
    projected, system, work, inverse, panel, panel_high_low = refs[7:]
    order = projected.shape[1]
    blocks = order // TILE
    width = out.shape[2]
    for slot in range(2):
        for distance in range(X_CHIPS):
            block = quarter(rows, slot, distance)
            size = block.shape[0]
            projected[slot, distance * size : (distance + 1) * size, :] = block

    def normal_equations(j, carry):
        for slot in range(2):
            columns = projected[slot, :, pl.ds(pl.multiple_of(j * TILE, TILE), TILE)].T
            system[slot, j, :, :order] = jnp.dot(columns, projected[slot], preferred_element_type=F32)
            right = jnp.dot(columns, back[slot], preferred_element_type=F32)
            system[slot, j, :, order:] = right[:, :width] + right[:, width:]
        return carry

    lax.fori_loop(0, blocks, normal_equations, 0)

    def step(j, carry):
        here = pl.ds(pl.multiple_of(j * TILE, TILE), TILE)
        for slot in range(2):
            work[slot] = system[slot, j, :, here]
        inverse_factors(work, inverse)
        for slot in range(2):
            high, low = high_low(inverse[slot])
            left = jnp.concatenate([high, high, low], axis=1)
            high, low = high_low(system[slot, j])
            right = jnp.concatenate([high, low, high], axis=0)
            solved = jnp.dot(left, right, preferred_element_type=F32)
            panel[slot] = solved
            high, low = high_low(solved)
            panel_high_low[slot] = jnp.concatenate([high, low, high], axis=0)
            out[slot, here, :] = jnp.where(live[slot] >= 0, solved[:, order:], 0.0)

        def trail(i, inner):
            for slot in range(2):
                columns = panel[slot, :, pl.ds(pl.multiple_of(i * TILE, TILE), TILE)].T
                high, low = high_low(columns)
                left = jnp.concatenate([high, high, low], axis=1)
                system[slot, i] -= jnp.dot(left, panel_high_low[slot], preferred_element_type=F32)
            return inner

        lax.fori_loop(j + 1, blocks, trail, 0)
        return carry

    lax.fori_loop(0, blocks, step, 0)


def back_moments(rows, moment):
    order, width = moment.shape[1:]
    return pl.pallas_call(
        back_kernel,
        out_shape=jax.ShapeDtypeStruct((2, order, 2 * width), BF16),
        compiler_params=pltpu.CompilerParams(vmem_limit_bytes=VMEM_BYTES),
        cost_estimate=pl.CostEstimate(flops=8 * order * order * width, bytes_accessed=6 << 20, transcendentals=0),
        name="back_moments",
    )(*rows, moment)


def project(place, factor, rows):
    smem = pl.BlockSpec(memory_space=pltpu.SMEM)
    vmem = pl.BlockSpec(memory_space=pltpu.VMEM)
    return pl.pallas_call(
        project_kernel,
        out_shape=jax.ShapeDtypeStruct(factor.shape, BF16),
        in_specs=[smem] + [vmem] * 6,
        out_specs=vmem,
        compiler_params=pltpu.CompilerParams(vmem_limit_bytes=VMEM_BYTES),
        cost_estimate=pl.CostEstimate(flops=2 * factor.size * factor.shape[2], bytes_accessed=5 << 20, transcendentals=0),
        name="project",
    )(place, factor, *rows)


def eliminate(live, rows, back):
    _, order, twice = back.shape
    width = twice // 2
    smem = pl.BlockSpec(memory_space=pltpu.SMEM)
    vmem = pl.BlockSpec(memory_space=pltpu.VMEM)
    return pl.pallas_call(
        eliminate_kernel,
        out_shape=jax.ShapeDtypeStruct((2, order, width), F32),
        in_specs=[smem] + [vmem] * 6,
        out_specs=vmem,
        scratch_shapes=[
            pltpu.VMEM((2, order, order), BF16),
            pltpu.VMEM((2, order // TILE, TILE, order + width), F32),
            pltpu.VMEM((2, TILE, TILE), F32),
            pltpu.VMEM((2, TILE, TILE), F32),
            pltpu.VMEM((2, TILE, order + width), F32),
            pltpu.VMEM((2, 3 * TILE, order + width), BF16),
        ],
        compiler_params=pltpu.CompilerParams(vmem_limit_bytes=VMEM_BYTES),
        cost_estimate=pl.CostEstimate(flops=6 * order**3, bytes_accessed=6 << 20, transcendentals=0),
        name="eliminate",
    )(live, *rows, back)


def on_device(partial_stats, old_basis, exp_avg, slot_block):
    slab_rows, order = partial_stats.shape[2:]
    n_rows = slot_block.shape[0]
    group = lax.axis_index("group")
    own_slots = lax.dynamic_index_in_dim(slot_block, lax.axis_index("dp"), 0, keepdims=False)
    live = (own_slots >= 0)[:, None, None]
    row = lax.broadcasted_iota(jnp.int32, (slab_rows, order), 0) + group * slab_rows
    column = lax.broadcasted_iota(jnp.int32, (slab_rows, order), 1)
    identity = (row == column).astype(F32)[None]

    previous = jnp.where(live, old_basis[0], identity.astype(BF16))
    previous_rows = gather_rows(previous)

    sent = jnp.take(partial_stats[0], jnp.maximum(slot_block.reshape(-1), 0), axis=0)
    sent = sent.reshape(n_rows, 2, slab_rows, order)
    shares = lax.all_to_all(sent, "dp", split_axis=0, concat_axis=0)
    factor = jnp.where(live, jnp.sum(shares.astype(F32), axis=0), identity).astype(BF16)

    place = jnp.stack([group // Z_CHIPS, group % Z_CHIPS]).astype(jnp.int32)
    projected_rows = gather_rows(project(place, factor, previous_rows))
    back = back_moments(previous_rows, exp_avg[0])
    return eliminate(own_slots, projected_rows, back)[None]


def solution(mesh):
    return jax.shard_map(
        on_device,
        mesh=mesh,
        in_specs=(
            P("dp", None, "group", None),
            P("dp", None, "group", None),
            P("dp", None, None, "group"),
            P(),
        ),
        out_specs=P("dp", None, None, "group"),
        check_vma=False,
    )
```

time: 1340 us -> 288 us (0.21)
  other arithmetic: 526 us -> 3.79 us
  waiting for transfers between devices: 610 us -> 107 us
  matrix products: 102 us -> 0 us
  starting transfers between devices: 0.26 us -> 94 us
  Pallas kernels: 0 us -> 76.3 us
  local copies, waits for them, and re-layouts: 70.1 us -> 5.41 us
  loops' own time: 14 us -> 0 us
    another operation x66 -> x1, other arithmetic: 513 us -> 0.08 us  [on_device(): place = jnp.stack([group // Z_CHIPS, group % Z_CHIPS]).astype(jnp.int32)]
    all_gather x6 -> x0, waiting for transfers between devices: 487 us -> none  [the longest x2 167 us: refresh_slot(): previous_full = lax.all_gather(previous, 'group', axis=0, tiled=True)]
    psum x1 -> x0, waiting for transfers between devices: 123 us -> none  [on_device(): lax.psum(local_stats.astype(jnp.float32).astype(jnp.bfloat16), 'dp')]
    ppermute x0 -> x24, starting transfers between devices: none -> 86.6 us  [from_neighbour(): return lax.ppermute(value, 'group', pairs)]
    pallas_call x0 -> x3, Pallas kernels: none -> 76.3 us  [the longest x1 71.4 us: eliminate(): pl.pallas_call(eliminate_kernel, out_shape=jax.ShapeDtypeStruct((2, order...]
    another operation x58 -> x0, matrix products: 68.8 us -> none  [the longest x28 46.1 us: refresh_slot(): lower_factor = jnp.linalg.cholesky(gram_total)]
    ppermute x0 -> x24, waiting for transfers between devices: none -> 58.2 us  [from_neighbour(): return lax.ppermute(value, 'group', pairs)]
    another operation x68 -> x4, local copies, waits for them, and re-layouts: 50.5 us -> 0.2 us  [gather_rows(): jnp.stack(pieces, axis=1).reshape(2, Z_CHIPS * slab.shape[1], slab.shape[2])]
  transfers between devices with their start and end apart: 7 -> 25, of which waited for: 7 -> 10; matrix products, arithmetic and copies ran while one was open for 0% -> 1% of each run, Pallas kernels for 0% -> 1%
where the time goes in v1:
time: 288 us; the launch traced here: 287 us
  waiting for transfers between devices  107 us (37%)
  starting transfers between devices  94 us (33%)
  Pallas kernels  76.3 us (26%)
  local copies, waits for them, and re-layouts  5.41 us (2%)
  other arithmetic  3.79 us (1%)
    ppermute x24, starting transfers between devices, from_neighbour(): return lax.ppermute(value, 'group', pairs)  86.6 us
    pallas_call x1, Pallas kernels, eliminate(): pl.pallas_call(eliminate_kernel, out_shape=jax.ShapeDtypeStruct((2, order...  71.4 us
    ppermute x24, waiting for transfers between devices, from_neighbour(): return lax.ppermute(value, 'group', pairs)  58.2 us
    all_to_all x1, waiting for transfers between devices, on_device(): shares = lax.all_to_all(sent, 'dp', split_axis=0, concat_axis=0)  48.9 us
    all_to_all x1, starting transfers between devices, on_device(): shares = lax.all_to_all(sent, 'dp', split_axis=0, concat_axis=0)  7.34 us
  transfers between devices with their start and end apart: 25, of which 10 were waited for; matrix products, arithmetic and copies ran while one was open for 1% of the time, Pallas kernels for 1%

profile of v1, /device:TPU:6, one launch (start us, length us, event | category | flops | bytes accessed | tf_op | source)
XLA Modules:
  0.0 287.2 jit_solution(8656556704961411706)
XLA Ops:
  4.0 7.3 %all-to-all-start = ((bf16[16,2,32,1024]{3,2,1,0:T(8,128)(2,1)}), bf16[16,2,32,1024]{3,2,1,0:T(8,128)(2,1)S(1)}, u32[]{:S(2)}, u32[]{:S(2)}) async-start(bf16[16,2,32,1024]{3,2,1,0:T(8,128)(2,1)} %broadcast_select_fusion), calls=%async_computation | async-start | bytes 4194304 | tf_op jit(solution)/shard_map/all_to_all | solution.py:253
  11.7 48.9 %all-to-all-done = bf16[16,2,32,1024]{3,2,1,0:T(8,128)(2,1)S(1)} async-done(((bf16[16,2,32,1024]{3,2,1,0:T(8,128)(2,1)}), bf16[16,2,32,1024]{3,2,1,0:T(8,128)(2,1)S(1)}, u32[]{:S(2)}, u32[]{:S(2)}) %all-to-all-start) | async-done | bytes 2097184 | tf_op jit(solution)/shard_map/all_to_all | solution.py:253
  61.0 6.1 %collective-permute-start.4 = (bf16[2,32,1024]{2,1,0:T(8,128)(2,1)S(1)}, bf16[2,32,1024]{2,1,0:T(8,128)(2,1)S(1)}, u32[]{:S(2)}, u32[]{:S(2)}) collective-permute-start(bf16[2,32,1024]{2,1,0:T(8,128)(2,1)S(1)} %get-tuple-element.5), channel_id=1, source_target_pairs={{6,0},{7,1},{0,2},{1,3},{2,4},{3,5},{4,6},{5,7},{14,8},{15,9},{8,1... | collective-permute-start | bytes 393224 | tf_op jit(solution)/shard_map/ppermute | solution.py:28
  67.1 6.8 %collective-permute-start.1 = (bf16[2,32,1024]{2,1,0:T(8,128)(2,1)S(1)}, bf16[2,32,1024]{2,1,0:T(8,128)(2,1)S(1)}, u32[]{:S(2)}, u32[]{:S(2)}) collective-permute-start(bf16[2,32,1024]{2,1,0:T(8,128)(2,1)S(1)} %get-tuple-element.5), channel_id=1, source_target_pairs={{2,0},{3,1},{4,2},{5,3},{6,4},{7,5},{0,6},{1,7},{10,8},{11,9},{12,... | collective-permute-start | bytes 393224 | tf_op jit(solution)/shard_map/ppermute | solution.py:28
  73.9 4.8 %collective-permute-start = (bf16[2,32,1024]{2,1,0:T(8,128)(2,1)S(1)}, bf16[2,32,1024]{2,1,0:T(8,128)(2,1)S(1)}, u32[]{:S(2)}, u32[]{:S(2)}) collective-permute-start(bf16[2,32,1024]{2,1,0:T(8,128)(2,1)S(1)} %get-tuple-element.5), channel_id=1, source_target_pairs={{1,0},{2,1},{3,2},{4,3},{5,4},{6,5},{7,6},{0,7},{9,8},{10,9},{11,1... | collective-permute-start | bytes 393224 | tf_op jit(solution)/shard_map/ppermute | solution.py:28
  82.7 6.0 %collective-permute-start.3 = (bf16[1,32,1024]{2,1,0:T(8,128)(2,1)S(1)}, bf16[1,32,1024]{2,1,0:T(8,128)(2,1)S(1)}, u32[]{:S(2)}, u32[]{:S(2)}) collective-permute-start(bf16[1,32,1024]{2,1,0:T(8,128)(2,1)S(1)} %slice.34), channel_id=1, source_target_pairs={{2,0},{3,1},{4,2},{5,3},{6,4},{7,5},{0,6},{1,7},{10,8},{11,9},{12,... | collective-permute-start | bytes 196616 | tf_op jit(solution)/shard_map/ppermute | solution.py:28
  88.8 2.5 collective-permute-start.6
  91.3 4.6 %collective-permute-start.2 = (bf16[2,32,1024]{2,1,0:T(8,128)(2,1)S(1)}, bf16[2,32,1024]{2,1,0:T(8,128)(2,1)S(1)}, u32[]{:S(2)}, u32[]{:S(2)}) collective-permute-start(bf16[2,32,1024]{2,1,0:T(8,128)(2,1)S(1)} %collective-permute-done.1), channel_id=1, source_target_pairs={{1,0},{2,1},{3,2},{4,3},{5,4},{6,5},{7,6},{0,7},{9,8},{10,9},{11,1... | collective-permute-start | bytes 393224 | tf_op jit(solution)/shard_map/ppermute | solution.py:28
  95.9 2.5 collective-permute-done.2
  98.6 2.4 collective-permute-start.10
  101.0 3.5 %collective-permute-start.8 = (bf16[2,256,1024]{2,1,0:T(8,128)(2,1)S(1)}, bf16[2,256,1024]{2,1,0:T(8,128)(2,1)S(1)}, u32[]{:S(2)}, u32[]{:S(2)}) collective-permute-start(bf16[2,256,1024]{2,1,0:T(8,128)(2,1)S(1)} %bitcast.58), channel_id=1, source_target_pairs={{8,0},{9,1},{10,2},{11,3},{12,4},{13,5},{14,6},{15,7},{16,8},{17,9... | collective-permute-start | bytes 3145736 | tf_op jit(solution)/shard_map/ppermute | solution.py:28
  104.5 18.7 %collective-permute-done.10.refs_4_ = bf16[2,256,1024]{2,1,0:T(8,128)(2,1)S(1)} collective-permute-done((bf16[2,256,1024]{2,1,0:T(8,128)(2,1)S(1)}, bf16[2,256,1024]{2,1,0:T(8,128)(2,1)S(1)}, u32[]{:S(2)}, u32[]{:S(2)}) %collective-permute-start.10) | collective-permute-done | bytes 1048608 | tf_op jit(solution)/shard_map/ppermute | solution.py:28
  124.0 3.6 %collective-permute-start.11 = (bf16[256,1024]{1,0:T(8,128)(2,1)}, bf16[256,1024]{1,0:T(8,128)(2,1)}, u32[]{:S(2)}, u32[]{:S(2)}) collective-permute-start(bf16[256,1024]{1,0:T(8,128)(2,1)} %slice_bitcast_fusion.2), channel_id=1, source_target_pairs={{24,0},{25,1},{26,2},{27,3},{28,4},{29,5},{30,6},{31,7},{0,8},{1,9... | collective-permute-start | bytes 1572872 | tf_op jit(solution)/shard_map/ppermute | solution.py:28
  129.4 2.2 collective-permute-start.9
  131.8 5.0 %collective-permute-done.11.refs_3_ = bf16[256,1024]{1,0:T(8,128)(2,1)} collective-permute-done((bf16[256,1024]{1,0:T(8,128)(2,1)}, bf16[256,1024]{1,0:T(8,128)(2,1)}, u32[]{:S(2)}, u32[]{:S(2)}) %collective-permute-start.11) | collective-permute-done | bytes 524320 | tf_op jit(solution)/shard_map/ppermute | solution.py:28
  136.8 6.3 %collective-permute-done.9.refs_2_ = bf16[256,1024]{1,0:T(8,128)(2,1)} collective-permute-done((bf16[256,1024]{1,0:T(8,128)(2,1)}, bf16[256,1024]{1,0:T(8,128)(2,1)}, u32[]{:S(2)}, u32[]{:S(2)}) %collective-permute-start.9) | collective-permute-done | bytes 524320 | tf_op jit(solution)/shard_map/ppermute | solution.py:28
  146.4 2.3 collective-permute-start.19
  148.7 5.2 %collective-permute-start.16 = (bf16[2,32,1024]{2,1,0:T(8,128)(2,1)S(1)}, bf16[2,32,1024]{2,1,0:T(8,128)(2,1)S(1)}, u32[]{:S(2)}, u32[]{:S(2)}) collective-permute-start(bf16[2,32,1024]{2,1,0:T(8,128)(2,1)S(1)} %project.1), channel_id=1, source_target_pairs={{6,0},{7,1},{0,2},{1,3},{2,4},{3,5},{4,6},{5,7},{14,8},{15,9},{8,1... | collective-permute-start | bytes 393224 | tf_op jit(solution)/shard_map/ppermute | solution.py:28
  153.9 2.9 collective-permute-start.13
  156.7 3.5 %collective-permute-start.12 = (bf16[2,32,1024]{2,1,0:T(8,128)(2,1)S(1)}, bf16[2,32,1024]{2,1,0:T(8,128)(2,1)S(1)}, u32[]{:S(2)}, u32[]{:S(2)}) collective-permute-start(bf16[2,32,1024]{2,1,0:T(8,128)(2,1)S(1)} %project.1), channel_id=1, source_target_pairs={{1,0},{2,1},{3,2},{4,3},{5,4},{6,5},{7,6},{0,7},{9,8},{10,9},{11,1... | collective-permute-start | bytes 393224 | tf_op jit(solution)/shard_map/ppermute | solution.py:28
  160.3 2.8 collective-permute-start.17
  163.6 4.7 %collective-permute-start.15 = (bf16[1,32,1024]{2,1,0:T(8,128)(2,1)S(1)}, bf16[1,32,1024]{2,1,0:T(8,128)(2,1)S(1)}, u32[]{:S(2)}, u32[]{:S(2)}) collective-permute-start(bf16[1,32,1024]{2,1,0:T(8,128)(2,1)S(1)} %slice.38), channel_id=1, source_target_pairs={{2,0},{3,1},{4,2},{5,3},{6,4},{7,5},{0,6},{1,7},{10,8},{11,9},{12,... | collective-permute-start | bytes 196616 | tf_op jit(solution)/shard_map/ppermute | solution.py:28
  168.3 2.3 collective-permute-start.18
  170.6 4.7 %collective-permute-start.14 = (bf16[2,32,1024]{2,1,0:T(8,128)(2,1)S(1)}, bf16[2,32,1024]{2,1,0:T(8,128)(2,1)S(1)}, u32[]{:S(2)}, u32[]{:S(2)}) collective-permute-start(bf16[2,32,1024]{2,1,0:T(8,128)(2,1)S(1)} %collective-permute-done.13), channel_id=1, source_target_pairs={{1,0},{2,1},{3,2},{4,3},{5,4},{6,5},{7,6},{0,7},{9,8},{10,9},{11,1... | collective-permute-start | bytes 393224 | tf_op jit(solution)/shard_map/ppermute | solution.py:28
  175.4 2.5 collective-permute-done.14
  180.2 3.9 %collective-permute-start.20 = (bf16[2,256,1024]{2,1,0:T(8,128)(2,1)S(1)}, bf16[2,256,1024]{2,1,0:T(8,128)(2,1)S(1)}, u32[]{:S(2)}, u32[]{:S(2)}) collective-permute-start(bf16[2,256,1024]{2,1,0:T(8,128)(2,1)S(1)} %bitcast.62), channel_id=1, source_target_pairs={{8,0},{9,1},{10,2},{11,3},{12,4},{13,5},{14,6},{15,7},{16,8},{17,9... | collective-permute-start | bytes 3145736 | tf_op jit(solution)/shard_map/ppermute | solution.py:28
  184.1 17.4 %collective-permute-done.22.refs_4_ = bf16[2,256,1024]{2,1,0:T(8,128)(2,1)S(1)} collective-permute-done((bf16[2,256,1024]{2,1,0:T(8,128)(2,1)S(1)}, bf16[2,256,1024]{2,1,0:T(8,128)(2,1)S(1)}, u32[]{:S(2)}, u32[]{:S(2)}) %collective-permute-start.22) | collective-permute-done | bytes 1048608 | tf_op jit(solution)/shard_map/ppermute | solution.py:28
  203.6 4.1 %collective-permute-start.21 = (bf16[256,1024]{1,0:T(8,128)(2,1)S(1)}, bf16[256,1024]{1,0:T(8,128)(2,1)S(1)}, u32[]{:S(2)}, u32[]{:S(2)}) collective-permute-start(bf16[256,1024]{1,0:T(8,128)(2,1)S(1)} %slice_bitcast_fusion.1), channel_id=1, source_target_pairs={{8,0},{9,1},{10,2},{11,3},{12,4},{13,5},{14,6},{15,7},{16,8},{17,9... | collective-permute-start | bytes 1572872 | tf_op jit(solution)/shard_map/ppermute | solution.py:28
  207.7 2.9 back_moments.1.refs_5_
  210.5 2.1 collective-permute-done.23.refs_3_
  212.6 3.2 %collective-permute-done.21.refs_2_ = bf16[256,1024]{1,0:T(8,128)(2,1)S(1)} collective-permute-done((bf16[256,1024]{1,0:T(8,128)(2,1)S(1)}, bf16[256,1024]{1,0:T(8,128)(2,1)S(1)}, u32[]{:S(2)}, u32[]{:S(2)}) %collective-permute-start.21) | collective-permute-done | bytes 524320 | tf_op jit(solution)/shard_map/ppermute | solution.py:28
  215.8 71.4 %eliminate.1 = f32[2,1024,128]{2,1,0:T(8,128)} custom-call(s32[2]{0:T(128)S(1)} %dynamic-slice_reduce_fusion.live, bf16[2,256,1024]{2,1,0:T(8,128)(2,1)S(1)} %bitcast.63, bf16[2,256,1024]{2,1,0:T(8,128)(2,1)S(1)} %collective-permute-done.20.refs_1_, bf16[256,1024]{1,0:T(8,128)(2,1)S(1)} %collective-permute-done.21.refs_2_, ...), custom_call_target="tpu_custom_call" | custom-call | flops 6442450944 | bytes 6291456 | tf_op jit(solution)/shard_map/eliminate/pallas_call | solution.py:219
  (74 shorter events, 19.6 us)
Async XLA Ops:
  0.0 1.7 copy-start
  4.0 7.4 %copy-start.5 = (s32[16,2]{0,1:T(2,128)S(1)}, s32[16,2]{0,1:T(2,128)}, u32[]{:S(2)}) copy-start(s32[16,2]{0,1:T(2,128)} %param.7) | copy-start | bytes 388
  4.0 56.5 %all-to-all-start = ((bf16[16,2,32,1024]{3,2,1,0:T(8,128)(2,1)}), bf16[16,2,32,1024]{3,2,1,0:T(8,128)(2,1)S(1)}, u32[]{:S(2)}, u32[]{:S(2)}) async-start(bf16[16,2,32,1024]{3,2,1,0:T(8,128)(2,1)} %broadcast_select_fusion), calls=%async_computation | async-start | bytes 4194304 | tf_op jit(solution)/shard_map/all_to_all | solution.py:253
  11.4 49.5 %copy-start.4 = (bf16[1,2,32,1024]{3,2,1,0:T(8,128)(2,1)S(1)}, bf16[1,2,32,1024]{3,2,1,0:T(8,128)(2,1)}, u32[]{:S(2)}) copy-start(bf16[1,2,32,1024]{3,2,1,0:T(8,128)(2,1)} %param.5) | copy-start | bytes 393220
  61.0 19.7 %collective-permute-start.4 = (bf16[2,32,1024]{2,1,0:T(8,128)(2,1)S(1)}, bf16[2,32,1024]{2,1,0:T(8,128)(2,1)S(1)}, u32[]{:S(2)}, u32[]{:S(2)}) collective-permute-start(bf16[2,32,1024]{2,1,0:T(8,128)(2,1)S(1)} %get-tuple-element.5), channel_id=1, source_target_pairs={{6,0},{7,1},{0,2},{1,3},{2,4},{3,5},{4,6},{5,7},{14,8},{15,9},{8,1... | collective-permute-start | bytes 393224 | tf_op jit(solution)/shard_map/ppermute | solution.py:28
  67.1 15.6 %collective-permute-start.1 = (bf16[2,32,1024]{2,1,0:T(8,128)(2,1)S(1)}, bf16[2,32,1024]{2,1,0:T(8,128)(2,1)S(1)}, u32[]{:S(2)}, u32[]{:S(2)}) collective-permute-start(bf16[2,32,1024]{2,1,0:T(8,128)(2,1)S(1)} %get-tuple-element.5), channel_id=1, source_target_pairs={{2,0},{3,1},{4,2},{5,3},{6,4},{7,5},{0,6},{1,7},{10,8},{11,9},{12,... | collective-permute-start | bytes 393224 | tf_op jit(solution)/shard_map/ppermute | solution.py:28
  73.9 17.4 %collective-permute-start = (bf16[2,32,1024]{2,1,0:T(8,128)(2,1)S(1)}, bf16[2,32,1024]{2,1,0:T(8,128)(2,1)S(1)}, u32[]{:S(2)}, u32[]{:S(2)}) collective-permute-start(bf16[2,32,1024]{2,1,0:T(8,128)(2,1)S(1)} %get-tuple-element.5), channel_id=1, source_target_pairs={{1,0},{2,1},{3,2},{4,3},{5,4},{6,5},{7,6},{0,7},{9,8},{10,9},{11,1... | collective-permute-start | bytes 393224 | tf_op jit(solution)/shard_map/ppermute | solution.py:28
  78.8 19.6 %collective-permute-start.7 = (bf16[2,32,1024]{2,1,0:T(8,128)(2,1)S(1)}, bf16[2,32,1024]{2,1,0:T(8,128)(2,1)S(1)}, u32[]{:S(2)}, u32[]{:S(2)}) collective-permute-start(bf16[2,32,1024]{2,1,0:T(8,128)(2,1)S(1)} %get-tuple-element.5), channel_id=1, source_target_pairs={{7,0},{0,1},{1,2},{2,3},{3,4},{4,5},{5,6},{6,7},{15,8},{8,9},{9,10... | collective-permute-start | bytes 393224 | tf_op jit(solution)/shard_map/ppermute | solution.py:28
  80.8 17.6 %collective-permute-start.5 = (bf16[1,32,1024]{2,1,0:T(8,128)(2,1)S(1)}, bf16[1,32,1024]{2,1,0:T(8,128)(2,1)S(1)}, u32[]{:S(2)}, u32[]{:S(2)}) collective-permute-start(bf16[1,32,1024]{2,1,0:T(8,128)(2,1)S(1)} %slice.35), channel_id=1, source_target_pairs={{6,0},{7,1},{0,2},{1,3},{2,4},{3,5},{4,6},{5,7},{14,8},{15,9},{8,1... | collective-permute-start | bytes 196616 | tf_op jit(solution)/shard_map/ppermute | solution.py:28
  82.7 15.6 %collective-permute-start.3 = (bf16[1,32,1024]{2,1,0:T(8,128)(2,1)S(1)}, bf16[1,32,1024]{2,1,0:T(8,128)(2,1)S(1)}, u32[]{:S(2)}, u32[]{:S(2)}) collective-permute-start(bf16[1,32,1024]{2,1,0:T(8,128)(2,1)S(1)} %slice.34), channel_id=1, source_target_pairs={{2,0},{3,1},{4,2},{5,3},{6,4},{7,5},{0,6},{1,7},{10,8},{11,9},{12,... | collective-permute-start | bytes 196616 | tf_op jit(solution)/shard_map/ppermute | solution.py:28
  88.8 9.6 %collective-permute-start.6 = (bf16[2,32,1024]{2,1,0:T(8,128)(2,1)S(1)}, bf16[2,32,1024]{2,1,0:T(8,128)(2,1)S(1)}, u32[]{:S(2)}, u32[]{:S(2)}) collective-permute-start(bf16[2,32,1024]{2,1,0:T(8,128)(2,1)S(1)} %collective-permute-done.4), channel_id=1, source_target_pairs={{7,0},{0,1},{1,2},{2,3},{3,4},{4,5},{5,6},{6,7},{15,8},{8,9},{9,10... | collective-permute-start | bytes 393224 | tf_op jit(solution)/shard_map/ppermute | solution.py:28
  91.3 7.1 %collective-permute-start.2 = (bf16[2,32,1024]{2,1,0:T(8,128)(2,1)S(1)}, bf16[2,32,1024]{2,1,0:T(8,128)(2,1)S(1)}, u32[]{:S(2)}, u32[]{:S(2)}) collective-permute-start(bf16[2,32,1024]{2,1,0:T(8,128)(2,1)S(1)} %collective-permute-done.1), channel_id=1, source_target_pairs={{1,0},{2,1},{3,2},{4,3},{5,4},{6,5},{7,6},{0,7},{9,8},{10,9},{11,1... | collective-permute-start | bytes 393224 | tf_op jit(solution)/shard_map/ppermute | solution.py:28
  98.6 24.6 %collective-permute-start.10 = (bf16[2,256,1024]{2,1,0:T(8,128)(2,1)S(1)}, bf16[2,256,1024]{2,1,0:T(8,128)(2,1)S(1)}, u32[]{:S(2)}, u32[]{:S(2)}) collective-permute-start(bf16[2,256,1024]{2,1,0:T(8,128)(2,1)S(1)} %bitcast.57), channel_id=1, source_target_pairs={{24,0},{25,1},{26,2},{27,3},{28,4},{29,5},{30,6},{31,7},{0,8},{1,9... | collective-permute-start | bytes 3145736 | tf_op jit(solution)/shard_map/ppermute | solution.py:28
  101.0 26.6 %collective-permute-start.8 = (bf16[2,256,1024]{2,1,0:T(8,128)(2,1)S(1)}, bf16[2,256,1024]{2,1,0:T(8,128)(2,1)S(1)}, u32[]{:S(2)}, u32[]{:S(2)}) collective-permute-start(bf16[2,256,1024]{2,1,0:T(8,128)(2,1)S(1)} %bitcast.58), channel_id=1, source_target_pairs={{8,0},{9,1},{10,2},{11,3},{12,4},{13,5},{14,6},{15,7},{16,8},{17,9... | collective-permute-start | bytes 3145736 | tf_op jit(solution)/shard_map/ppermute | solution.py:28
  124.0 12.8 %collective-permute-start.11 = (bf16[256,1024]{1,0:T(8,128)(2,1)}, bf16[256,1024]{1,0:T(8,128)(2,1)}, u32[]{:S(2)}, u32[]{:S(2)}) collective-permute-start(bf16[256,1024]{1,0:T(8,128)(2,1)} %slice_bitcast_fusion.2), channel_id=1, source_target_pairs={{24,0},{25,1},{26,2},{27,3},{28,4},{29,5},{30,6},{31,7},{0,8},{1,9... | collective-permute-start | bytes 1572872 | tf_op jit(solution)/shard_map/ppermute | solution.py:28
  128.5 1.0 copy-start.1
  129.4 13.7 %collective-permute-start.9 = (bf16[256,1024]{1,0:T(8,128)(2,1)}, bf16[256,1024]{1,0:T(8,128)(2,1)}, u32[]{:S(2)}, u32[]{:S(2)}) collective-permute-start(bf16[256,1024]{1,0:T(8,128)(2,1)} %slice_bitcast_fusion.3), channel_id=1, source_target_pairs={{8,0},{9,1},{10,2},{11,3},{12,4},{13,5},{14,6},{15,7},{16,8},{17,9... | collective-permute-start | bytes 1572872 | tf_op jit(solution)/shard_map/ppermute | solution.py:28
  143.1 1.2 copy-start.2
  146.4 31.5 %collective-permute-start.19 = (bf16[2,32,1024]{2,1,0:T(8,128)(2,1)S(1)}, bf16[2,32,1024]{2,1,0:T(8,128)(2,1)S(1)}, u32[]{:S(2)}, u32[]{:S(2)}) collective-permute-start(bf16[2,32,1024]{2,1,0:T(8,128)(2,1)S(1)} %project.1), channel_id=1, source_target_pairs={{7,0},{0,1},{1,2},{2,3},{3,4},{4,5},{5,6},{6,7},{15,8},{8,9},{9,10... | collective-permute-start | bytes 393224 | tf_op jit(solution)/shard_map/ppermute | solution.py:28
  148.7 11.6 %collective-permute-start.16 = (bf16[2,32,1024]{2,1,0:T(8,128)(2,1)S(1)}, bf16[2,32,1024]{2,1,0:T(8,128)(2,1)S(1)}, u32[]{:S(2)}, u32[]{:S(2)}) collective-permute-start(bf16[2,32,1024]{2,1,0:T(8,128)(2,1)S(1)} %project.1), channel_id=1, source_target_pairs={{6,0},{7,1},{0,2},{1,3},{2,4},{3,5},{4,6},{5,7},{14,8},{15,9},{8,1... | collective-permute-start | bytes 393224 | tf_op jit(solution)/shard_map/ppermute | solution.py:28
  153.9 9.7 %collective-permute-start.13 = (bf16[2,32,1024]{2,1,0:T(8,128)(2,1)S(1)}, bf16[2,32,1024]{2,1,0:T(8,128)(2,1)S(1)}, u32[]{:S(2)}, u32[]{:S(2)}) collective-permute-start(bf16[2,32,1024]{2,1,0:T(8,128)(2,1)S(1)} %project.1), channel_id=1, source_target_pairs={{2,0},{3,1},{4,2},{5,3},{6,4},{7,5},{0,6},{1,7},{10,8},{11,9},{12,... | collective-permute-start | bytes 393224 | tf_op jit(solution)/shard_map/ppermute | solution.py:28
  156.7 13.9 %collective-permute-start.12 = (bf16[2,32,1024]{2,1,0:T(8,128)(2,1)S(1)}, bf16[2,32,1024]{2,1,0:T(8,128)(2,1)S(1)}, u32[]{:S(2)}, u32[]{:S(2)}) collective-permute-start(bf16[2,32,1024]{2,1,0:T(8,128)(2,1)S(1)} %project.1), channel_id=1, source_target_pairs={{1,0},{2,1},{3,2},{4,3},{5,4},{6,5},{7,6},{0,7},{9,8},{10,9},{11,1... | collective-permute-start | bytes 393224 | tf_op jit(solution)/shard_map/ppermute | solution.py:28
  160.3 17.6 %collective-permute-start.17 = (bf16[1,32,1024]{2,1,0:T(8,128)(2,1)S(1)}, bf16[1,32,1024]{2,1,0:T(8,128)(2,1)S(1)}, u32[]{:S(2)}, u32[]{:S(2)}) collective-permute-start(bf16[1,32,1024]{2,1,0:T(8,128)(2,1)S(1)} %slice.39), channel_id=1, source_target_pairs={{6,0},{7,1},{0,2},{1,3},{2,4},{3,5},{4,6},{5,7},{14,8},{15,9},{8,1... | collective-permute-start | bytes 196616 | tf_op jit(solution)/shard_map/ppermute | solution.py:28
  163.6 14.3 %collective-permute-start.15 = (bf16[1,32,1024]{2,1,0:T(8,128)(2,1)S(1)}, bf16[1,32,1024]{2,1,0:T(8,128)(2,1)S(1)}, u32[]{:S(2)}, u32[]{:S(2)}) collective-permute-start(bf16[1,32,1024]{2,1,0:T(8,128)(2,1)S(1)} %slice.38), channel_id=1, source_target_pairs={{2,0},{3,1},{4,2},{5,3},{6,4},{7,5},{0,6},{1,7},{10,8},{11,9},{12,... | collective-permute-start | bytes 196616 | tf_op jit(solution)/shard_map/ppermute | solution.py:28
  168.3 9.6 %collective-permute-start.18 = (bf16[2,32,1024]{2,1,0:T(8,128)(2,1)S(1)}, bf16[2,32,1024]{2,1,0:T(8,128)(2,1)S(1)}, u32[]{:S(2)}, u32[]{:S(2)}) collective-permute-start(bf16[2,32,1024]{2,1,0:T(8,128)(2,1)S(1)} %collective-permute-done.16), channel_id=1, source_target_pairs={{7,0},{0,1},{1,2},{2,3},{3,4},{4,5},{5,6},{6,7},{15,8},{8,9},{9,10... | collective-permute-start | bytes 393224 | tf_op jit(solution)/shard_map/ppermute | solution.py:28
  170.6 7.2 %collective-permute-start.14 = (bf16[2,32,1024]{2,1,0:T(8,128)(2,1)S(1)}, bf16[2,32,1024]{2,1,0:T(8,128)(2,1)S(1)}, u32[]{:S(2)}, u32[]{:S(2)}) collective-permute-start(bf16[2,32,1024]{2,1,0:T(8,128)(2,1)S(1)} %collective-permute-done.13), channel_id=1, source_target_pairs={{1,0},{2,1},{3,2},{4,3},{5,4},{6,5},{7,6},{0,7},{9,8},{10,9},{11,1... | collective-permute-start | bytes 393224 | tf_op jit(solution)/shard_map/ppermute | solution.py:28
  178.0 29.7 %copy-start.3 = (bf16[2,256,1024]{2,1,0:T(8,128)(2,1)S(1)}, bf16[2,256,1024]{2,1,0:T(8,128)(2,1)}, u32[]{:S(2)}) copy-start(bf16[2,256,1024]{2,1,0:T(8,128)(2,1)} %copy-done.1) | copy-start | bytes 3145732
  178.1 23.4 %collective-permute-start.22 = (bf16[2,256,1024]{2,1,0:T(8,128)(2,1)S(1)}, bf16[2,256,1024]{2,1,0:T(8,128)(2,1)S(1)}, u32[]{:S(2)}, u32[]{:S(2)}) collective-permute-start(bf16[2,256,1024]{2,1,0:T(8,128)(2,1)S(1)} %bitcast.61), channel_id=1, source_target_pairs={{24,0},{25,1},{26,2},{27,3},{28,4},{29,5},{30,6},{31,7},{0,8},{1,9... | collective-permute-start | bytes 3145736 | tf_op jit(solution)/shard_map/ppermute | solution.py:28
  180.2 23.3 %collective-permute-start.20 = (bf16[2,256,1024]{2,1,0:T(8,128)(2,1)S(1)}, bf16[2,256,1024]{2,1,0:T(8,128)(2,1)S(1)}, u32[]{:S(2)}, u32[]{:S(2)}) collective-permute-start(bf16[2,256,1024]{2,1,0:T(8,128)(2,1)S(1)} %bitcast.62), channel_id=1, source_target_pairs={{8,0},{9,1},{10,2},{11,3},{12,4},{13,5},{14,6},{15,7},{16,8},{17,9... | collective-permute-start | bytes 3145736 | tf_op jit(solution)/shard_map/ppermute | solution.py:28
  201.6 11.1 %collective-permute-start.23 = (bf16[256,1024]{1,0:T(8,128)(2,1)S(1)}, bf16[256,1024]{1,0:T(8,128)(2,1)S(1)}, u32[]{:S(2)}, u32[]{:S(2)}) collective-permute-start(bf16[256,1024]{1,0:T(8,128)(2,1)S(1)} %slice_bitcast_fusion), channel_id=1, source_target_pairs={{24,0},{25,1},{26,2},{27,3},{28,4},{29,5},{30,6},{31,7},{0,8},{1,9... | collective-permute-start | bytes 1572872 | tf_op jit(solution)/shard_map/ppermute | solution.py:28
  203.6 12.3 %collective-permute-start.21 = (bf16[256,1024]{1,0:T(8,128)(2,1)S(1)}, bf16[256,1024]{1,0:T(8,128)(2,1)S(1)}, u32[]{:S(2)}, u32[]{:S(2)}) collective-permute-start(bf16[256,1024]{1,0:T(8,128)(2,1)S(1)} %slice_bitcast_fusion.1), channel_id=1, source_target_pairs={{8,0},{9,1},{10,2},{11,3},{12,4},{13,5},{14,6},{15,7},{16,8},{17,9... | collective-permute-start | bytes 1572872 | tf_op jit(solution)/shard_map/ppermute | solution.py:28

commit v2 on v1

v2 whole, which is shorter than its diff:
```python
import functools

import jax
import jax.numpy as jnp
from jax import lax
from jax.experimental import pallas as pl
from jax.experimental.pallas import tpu as pltpu
from jax.sharding import PartitionSpec as P

BF16, F32 = jnp.bfloat16, jnp.float32
VMEM_BYTES = 48 * 1024 * 1024
TILE = 128
SUB = 8
X_CHIPS, Z_CHIPS = 4, 8


def high_low(value):
    high = value.astype(BF16)
    return high, (value - high.astype(F32)).astype(BF16)


def from_neighbour(value, dx, dz):
    pairs = []
    for x in range(X_CHIPS):
        for z in range(Z_CHIPS):
            source = (x + dx) % X_CHIPS * Z_CHIPS + (z + dz) % Z_CHIPS
            pairs.append((source, x * Z_CHIPS + z))
    return lax.ppermute(value, "group", pairs)


def gather_factor(slab):
    rows_of_z = [[x * Z_CHIPS + z for z in range(Z_CHIPS)] for x in range(X_CHIPS)]
    copies = jnp.broadcast_to(slab[None], (Z_CHIPS,) + slab.shape)
    own = lax.all_to_all(copies, "group", split_axis=0, concat_axis=0, axis_index_groups=rows_of_z)
    after = from_neighbour(own, 1, 0)
    before = from_neighbour(own, -1, 0)
    half = Z_CHIPS // 2
    across_low = from_neighbour(after[:half], 1, 0)
    across_high = from_neighbour(before[half:], -1, 0)
    return own, after, across_low, across_high, before


def back_kernel(basis, moment, out):
    width = moment.shape[2]
    order = out.shape[1]
    for slot in range(2):
        high, low = high_low(moment[slot])
        both = jnp.concatenate([high, low], axis=1)
        product = jnp.dot(basis[:, slot].reshape(order, order), both, preferred_element_type=F32)
        high, low = high_low(product[:, :width] + product[:, width:])
        out[slot] = jnp.concatenate([high, low], axis=1)


def fill_factor(x, pieces, factor):
    own, after, across_low, across_high, before = pieces
    half = Z_CHIPS // 2
    blocks = factor.shape[1] // TILE
    for distance in range(X_CHIPS):
        for z_half in range(2):
            block_row = lax.rem(x + distance, X_CHIPS) * 2 + z_half
            here = pl.ds(pl.multiple_of(block_row * TILE, TILE), TILE)
            for slot in range(2):
                if distance == 2:
                    piece = (across_low, across_high)[z_half][:, slot]
                else:
                    piece = (own, after, None, before)[distance][half * z_half : half * (z_half + 1), slot]
                piece = piece.reshape(TILE, piece.shape[2])
                for k in range(blocks // 2 + 1):
                    there = pl.ds(pl.multiple_of(lax.rem(block_row + k, blocks) * TILE, TILE), TILE)
                    block = piece[:, TILE * k : TILE * (k + 1)]
                    factor[slot, here, there] = block
                    if 0 < k < blocks // 2:
                        factor[slot, there, here] = block.T


def row_of(value, at):
    return jnp.broadcast_to(value[at : at + 1, :], value.shape)


def lane_of(value, at):
    return jnp.broadcast_to(value[:, at : at + 1], value.shape)


def inverse_factors(work, inverse):
    lane = lax.broadcasted_iota(jnp.int32, (SUB, TILE), 1)
    upper_half = lax.broadcasted_iota(jnp.int32, (SUB, TILE), 0) < SUB // 2
    n_sub = TILE // SUB
    tiles = [[work[slot, SUB * i : SUB * (i + 1), :] for i in range(n_sub)] for slot in range(2)]
    for s in range(n_sub):
        first = SUB * s
        inside = (lane >= first) & (lane < first + SUB)
        rows = [jnp.where(upper_half, row_of(tiles[0][s], r), row_of(tiles[1][s], r)) for r in range(SUB)]
        entry = [[lane_of(rows[r], first + c) for c in range(r + 1)] for r in range(SUB)]
        rows = [jnp.where(inside, jnp.where(lane == first + r, 1.0, 0.0), rows[r]) for r in range(SUB)]
        ratio = [[None] * SUB for _ in range(SUB)]
        inverse_pivot = [None] * SUB
        for k in range(SUB):
            inverse_pivot[k] = pl.reciprocal(entry[k][k], approx=True)
            for r in range(k + 1, SUB):
                ratio[r][k] = entry[r][k] * inverse_pivot[k]
            for r in range(k + 1, SUB):
                for c in range(k + 1, r + 1):
                    entry[r][c] = entry[r][c] - ratio[r][k] * entry[c][k]
                rows[r] = rows[r] - ratio[r][k] * rows[k]
        solved = [None] * SUB
        for k in reversed(range(SUB)):
            value = rows[k] * inverse_pivot[k]
            for r in reversed(range(k + 1, SUB)):
                value = value - ratio[r][k] * solved[r]
            solved[k] = value
        for k in range(SUB):
            scaled = jnp.where(lane < first + SUB, rows[k] * lax.rsqrt(entry[k][k]), 0.0)
            for slot in range(2):
                at = slot * (SUB // 2)
                inverse[slot, first + k : first + k + 1, :] = scaled[at : at + 1, :]
        if s + 1 == n_sub:
            break
        for slot in range(2):
            spread = [row_of(solved[k], slot * (SUB // 2)) for k in range(SUB)]
            for i in range(s + 1, n_sub):
                old = tiles[slot][i]
                terms = [lane_of(old, first + c) * spread[c] for c in range(SUB)]
                while len(terms) > 1:
                    terms = [a + b for a, b in zip(terms[::2], terms[1::2])]
                tiles[slot][i] = jnp.where(inside, 0.0, old) - terms[0]


def normal_equations(basis, back, factor, projected, transposed, system):
    order = factor.shape[1]
    width = back.shape[2] // 2
    chunk = 2 * TILE
    for slot in range(2):
        for at in range(0, order, chunk):
            columns = basis[:, slot, :, at : at + chunk].reshape(order, chunk)
            product = jnp.dot(factor[slot], columns, preferred_element_type=F32).astype(BF16)
            projected[slot, :, at : at + chunk] = product
            transposed[slot, at : at + chunk, :] = product.T
        for at in range(0, order, chunk):
            end = at + chunk
            product = jnp.dot(transposed[slot, :end, :], projected[slot, :, at:end], preferred_element_type=F32)
            system[slot, : end // TILE, :, at:end] = product.reshape(end // TILE, TILE, chunk)
        product = jnp.dot(transposed[slot], back[slot], preferred_element_type=F32)
        product = product[:, :width] + product[:, width:]
        system[slot, :, :, order:] = product.reshape(order // TILE, TILE, width)


def finish_block(block, live, inverse, system, out):
    order = out.shape[1]
    first = TILE * (block + 1)
    below = order - first
    for slot in range(2):
        high, low = high_low(inverse[slot])
        left = jnp.concatenate([high, high, low], axis=1)
        high, low = high_low(system[slot, block, :, first:])
        right = jnp.concatenate([high, low, high], axis=0)
        solved = jnp.dot(left, right, preferred_element_type=F32)
        out[slot, first - TILE : first, :] = jnp.where(live[slot] >= 0, solved[:, below:], 0.0)
        if below == 0:
            continue
        high, low = high_low(solved)
        right = jnp.concatenate([high, low, high], axis=0)
        high, low = high_low(solved[:, :below].T)
        left = jnp.concatenate([high, high, low], axis=1)
        end = right.shape[1]
        while end > 0:
            start = max(end - 2 * TILE, 0)
            rows = min(end, below)
            product = jnp.dot(left[:rows], right[:, start:end], preferred_element_type=F32)
            product = product.reshape(rows // TILE, TILE, end - start)
            system[slot, block + 1 : block + 1 + rows // TILE, :, first + start : first + end] -= product
            end = start


def eliminate_kernel(live, place, *refs):
    pieces, basis, back, out = refs[:5], refs[5], refs[6], refs[7]
    factor, projected, transposed, system, work, inverse = refs[8:]
    blocks = out.shape[1] // TILE
    fill_factor(place[0], pieces, factor)
    normal_equations(basis, back, factor, projected, transposed, system)

    def step(j, carry):
        for slot in range(2):
            work[slot] = system[slot, j, :, pl.ds(pl.multiple_of(j * TILE, TILE), TILE)]
        inverse_factors(work, inverse)
        for block in range(blocks):
            pl.when(j == block)(functools.partial(finish_block, block, live, inverse, system, out))
        return carry

    lax.fori_loop(0, blocks, step, 0)


def back_moments(basis, moment):
    order, width = moment.shape[1:]
    return pl.pallas_call(
        back_kernel,
        out_shape=jax.ShapeDtypeStruct((2, order, 2 * width), BF16),
        compiler_params=pltpu.CompilerParams(vmem_limit_bytes=VMEM_BYTES),
        cost_estimate=pl.CostEstimate(flops=8 * order * order * width, bytes_accessed=6 << 20, transcendentals=0),
        name="back_moments",
    )(basis, moment)


def eliminate(live, place, pieces, basis, back):
    _, order, twice = back.shape
    width = twice // 2
    smem = pl.BlockSpec(memory_space=pltpu.SMEM)
    vmem = pl.BlockSpec(memory_space=pltpu.VMEM)
    return pl.pallas_call(
        eliminate_kernel,
        out_shape=jax.ShapeDtypeStruct((2, order, width), F32),
        in_specs=[smem, smem] + [vmem] * 7,
        out_specs=vmem,
        scratch_shapes=[
            pltpu.VMEM((2, order, order), BF16),
            pltpu.VMEM((2, order, order), BF16),
            pltpu.VMEM((2, order, order), BF16),
            pltpu.VMEM((2, order // TILE, TILE, order + width), F32),
            pltpu.VMEM((2, TILE, TILE), F32),
            pltpu.VMEM((2, TILE, TILE), F32),
        ],
        compiler_params=pltpu.CompilerParams(vmem_limit_bytes=VMEM_BYTES),
        cost_estimate=pl.CostEstimate(flops=10 * order**3, bytes_accessed=12 << 20, transcendentals=0),
        name="eliminate",
    )(live, place, *pieces, basis, back)


def on_device(partial_stats, old_basis, exp_avg, slot_block):
    slab_rows, order = partial_stats.shape[2:]
    n_rows = slot_block.shape[0]
    group = lax.axis_index("group")
    own_slots = lax.dynamic_index_in_dim(slot_block, lax.axis_index("dp"), 0, keepdims=False)
    live = (own_slots >= 0)[:, None, None]
    row = lax.broadcasted_iota(jnp.int32, (slab_rows, order), 0) + group * slab_rows
    column = lax.broadcasted_iota(jnp.int32, (slab_rows, order), 1)

    previous = jnp.where(live, old_basis[0], (row == column).astype(BF16)[None])
    basis = lax.all_gather(previous, "group", axis=0)
    back = back_moments(basis, exp_avg[0])

    kept = order // 2 + TILE
    block_start = group * slab_rows // TILE * TILE
    stats = jnp.concatenate([partial_stats[0], partial_stats[0, :, :, : kept - TILE]], axis=2)
    stats = lax.dynamic_slice_in_dim(stats, block_start, kept, axis=2)
    sent = jnp.take(stats, jnp.maximum(slot_block.reshape(-1), 0), axis=0)
    sent = sent.reshape(n_rows, 2, slab_rows, kept)
    shares = lax.all_to_all(sent, "dp", split_axis=0, concat_axis=0)
    identity = (row[:, :kept] == column[:, :kept] + block_start).astype(F32)[None]
    factor = jnp.where(live, jnp.sum(shares.astype(F32), axis=0), identity).astype(BF16)

    place = jnp.stack([group // Z_CHIPS, group % Z_CHIPS]).astype(jnp.int32)
    return eliminate(own_slots, place, gather_factor(factor), basis, back)[None]


def solution(mesh):
    return jax.shard_map(
        on_device,
        mesh=mesh,
        in_specs=(
            P("dp", None, "group", None),
            P("dp", None, "group", None),
            P("dp", None, None, "group"),
            P(),
        ),
        out_specs=P("dp", None, None, "group"),
        check_vma=False,
    )
```

time: 288 us -> 198 us (0.69)
  starting transfers between devices: 94 us -> 19.3 us
  waiting for transfers between devices: 107 us -> 54.7 us
  blocking collectives: 0 us -> 35.8 us
  between operations: 0.62 us -> 13.6 us
  Pallas kernels: 76.3 us -> 64 us
    ppermute x24 -> x4, starting transfers between devices: 86.6 us -> 12.1 us  [from_neighbour(): return lax.ppermute(value, 'group', pairs)]
    all_to_all x0 -> x1, blocking collectives: none -> 35.8 us  [gather_factor(): lax.all_to_all(copies, 'group', split_axis=0, concat_axis=0, axis_index_g...]
    ppermute x24 -> x4, waiting for transfers between devices: 58.2 us -> 22.5 us  [from_neighbour(): return lax.ppermute(value, 'group', pairs)]
    all_to_all x1, waiting for transfers between devices: 48.9 us -> 32.1 us  [on_device(): shares = lax.all_to_all(sent, 'dp', split_axis=0, concat_axis=0)]
    pallas_call x1, Pallas kernels: 71.4 us -> 60.6 us  [eliminate(): pl.pallas_call(eliminate_kernel, out_shape=jax.ShapeDtypeStruct((2, order...]
  transfers between devices with their start and end apart: 25 -> 6, of which waited for: 10 -> 4; matrix products, arithmetic and copies ran while one was open for 1% -> 4% of each run, Pallas kernels for 1% -> 2%
where the time goes in v2:
time: 198 us; the launch traced here: 197 us
  Pallas kernels  64 us (32%)
  waiting for transfers between devices  54.7 us (28%)
  blocking collectives  35.8 us (18%)
  starting transfers between devices  19.3 us (10%)
  between operations  13.6 us (7%)
  other arithmetic  5.07 us (3%)
  local copies, waits for them, and re-layouts  4.66 us (2%)
    pallas_call x1, Pallas kernels, eliminate(): pl.pallas_call(eliminate_kernel, out_shape=jax.ShapeDtypeStruct((2, order...  60.6 us
    all_to_all x1, blocking collectives, gather_factor(): lax.all_to_all(copies, 'group', split_axis=0, concat_axis=0, axis_index_g...  35.8 us
    all_to_all x1, waiting for transfers between devices, on_device(): shares = lax.all_to_all(sent, 'dp', split_axis=0, concat_axis=0)  32.1 us
    ppermute x4, waiting for transfers between devices, from_neighbour(): return lax.ppermute(value, 'group', pairs)  22.5 us
    ppermute x4, starting transfers between devices, from_neighbour(): return lax.ppermute(value, 'group', pairs)  12.1 us
    all_to_all x1, starting transfers between devices, on_device(): shares = lax.all_to_all(sent, 'dp', split_axis=0, concat_axis=0)  7.21 us
  transfers between devices with their start and end apart: 6, of which 4 were waited for; matrix products, arithmetic and copies ran while one was open for 4% of the time, Pallas kernels for 2%

profile of v2, /device:TPU:6, one launch (start us, length us, event | category | flops | bytes accessed | tf_op | source)
XLA Modules:
  0.0 197.1 jit_solution(17337419470694665626)
XLA Ops:
  6.5 0.9 dynamic-slice_reduce_fusion.live
  7.5 0.1 fusion.1
  7.6 1.6 broadcast_select_fusion.1
  9.2 0.0 all-gather.2.cloned.1.call-update
  9.3 0.7 broadcast_compare_fusion
  10.0 0.1 copy.9
  10.1 0.7 broadcast_maximum_fusion
  10.7 0.1 copy.10
  10.8 0.1 reshape.48
  10.9 1.1 slice_bitcast_fusion
  12.0 0.3 fusion
  12.3 0.8 gather_fusion
  13.1 1.3 broadcast_select_fusion
  14.4 7.2 %all-to-all-start = ((bf16[16,2,32,640]{3,2,1,0:T(8,128)(2,1)}), bf16[16,2,32,640]{3,2,1,0:T(8,128)(2,1)S(1)}, u32[]{:S(2)}, u32[]{:S(2)}) async-start(bf16[16,2,32,640]{3,2,1,0:T(8,128)(2,1)} %broadcast_select_fusion), calls=%async_computation | async-start | bytes 2621440 | tf_op jit(solution)/shard_map/all_to_all | solution.py:246
  21.6 0.1 fusion.3
  21.7 32.1 %all-to-all-done = bf16[16,2,32,640]{3,2,1,0:T(8,128)(2,1)S(1)} async-done(((bf16[16,2,32,640]{3,2,1,0:T(8,128)(2,1)}), bf16[16,2,32,640]{3,2,1,0:T(8,128)(2,1)S(1)}, u32[]{:S(2)}, u32[]{:S(2)}) %all-to-all-start) | async-done | bytes 1310752 | tf_op jit(solution)/shard_map/all_to_all | solution.py:246
  53.8 0.2 convert_reduce_fusion
  54.0 0.1 select_convert_fusion
  54.0 0.1 broadcast_in_dim.58
  54.1 35.8 %all_to_all.10.refs_0_ = bf16[8,2,32,640]{3,2,1,0:T(8,128)(2,1)S(1)} all-to-all(bf16[8,2,32,640]{3,2,1,0:T(8,128)(2,1)S(1)} %broadcast_in_dim.58), channel_id=1, replica_groups={{0,1,2,3,4,5,6,7},{8,9,10,11,12,13,14,15},{16,17,18,19,20,21,22,23},{24..., dimensions={0} | all-to-all | bytes 1310720 | tf_op jit(solution)/shard_map/all_to_all | solution.py:34
  89.9 2.3 %collective-permute-start.2 = (bf16[8,2,32,640]{3,2,1,0:T(8,128)(2,1)S(1)}, bf16[8,2,32,640]{3,2,1,0:T(8,128)(2,1)S(1)}, u32[]{:S(2)}, u32[]{:S(2)}) collective-permute-start(bf16[8,2,32,640]{3,2,1,0:T(8,128)(2,1)S(1)} %all_to_all.10.refs_0_), channel_id=1, source_target_pairs={{24,0},{25,1},{26,2},{27,3},{28,4},{29,5},{30,6},{31,7},{0,8},{1,9... | collective-permute-start | bytes 1966088 | tf_op jit(solution)/shard_map/ppermute | solution.py:28
  92.3 3.5 %collective-permute-start = (bf16[8,2,32,640]{3,2,1,0:T(8,128)(2,1)S(1)}, bf16[8,2,32,640]{3,2,1,0:T(8,128)(2,1)S(1)}, u32[]{:S(2)}, u32[]{:S(2)}) collective-permute-start(bf16[8,2,32,640]{3,2,1,0:T(8,128)(2,1)S(1)} %all_to_all.10.refs_0_), channel_id=1, source_target_pairs={{8,0},{9,1},{10,2},{11,3},{12,4},{13,5},{14,6},{15,7},{16,8},{17,9... | collective-permute-start | bytes 1966088 | tf_op jit(solution)/shard_map/ppermute | solution.py:28
  95.8 15.5 %collective-permute-done.2.refs_4_ = bf16[8,2,32,640]{3,2,1,0:T(8,128)(2,1)S(1)} collective-permute-done((bf16[8,2,32,640]{3,2,1,0:T(8,128)(2,1)S(1)}, bf16[8,2,32,640]{3,2,1,0:T(8,128)(2,1)S(1)}, u32[]{:S(2)}, u32[]{:S(2)}) %collective-permute-start.2) | collective-permute-done | bytes 655392 | tf_op jit(solution)/shard_map/ppermute | solution.py:28
  111.3 0.8 slice.23
  112.0 4.3 %collective-permute-start.3 = (bf16[4,2,32,640]{3,2,1,0:T(8,128)(2,1)}, bf16[4,2,32,640]{3,2,1,0:T(8,128)(2,1)S(1)}, u32[]{:S(2)}, u32[]{:S(2)}) collective-permute-start(bf16[4,2,32,640]{3,2,1,0:T(8,128)(2,1)} %slice.23), channel_id=1, source_target_pairs={{24,0},{25,1},{26,2},{27,3},{28,4},{29,5},{30,6},{31,7},{0,8},{1,9... | collective-permute-start | bytes 983048 | tf_op jit(solution)/shard_map/ppermute | solution.py:28
  116.4 0.8 slice.22
  117.1 1.9 collective-permute-start.1
  119.1 0.1 pad_add_fusion.place
  119.2 3.4 %back_moments.1.refs_6_ = bf16[2,1024,256]{2,1,0:T(8,128)(2,1)S(1)} custom-call(bf16[32,2,32,1024]{3,2,1,0:T(8,128)(2,1)} %all-gather.2.cloned.1.call-done.basis.refs_5_, f32[2,1024,128]{2,1,0:T(8,128)S(1)} %bitcast.8), custom_call_target="tpu_custom_call" | custom-call | flops 1073741824 | bytes 6291456 | tf_op jit(solution)/shard_map/back_moments/pallas_call | solution.py:194
  122.6 1.0 collective-permute-done.3.refs_3_
  123.6 6.1 %collective-permute-done.1.refs_2_ = bf16[4,2,32,640]{3,2,1,0:T(8,128)(2,1)} collective-permute-done((bf16[4,2,32,640]{3,2,1,0:T(8,128)(2,1)}, bf16[4,2,32,640]{3,2,1,0:T(8,128)(2,1)}, u32[]{:S(2)}, u32[]{:S(2)}) %collective-permute-start.1) | collective-permute-done | bytes 327712 | tf_op jit(solution)/shard_map/ppermute | solution.py:28
  129.7 60.6 %eliminate.1 = f32[2,1024,128]{2,1,0:T(8,128)} custom-call(s32[2]{0:T(128)S(1)} %dynamic-slice_reduce_fusion.live, s32[2]{0:T(128)S(1)} %pad_add_fusion.place, bf16[8,2,32,640]{3,2,1,0:T(8,128)(2,1)S(1)} %all_to_all.10.refs_0_, bf16[8,2,32,640]{3,2,1,0:T(8,128)(2,1)S(1)} %collective-permute-done.refs_1_, ...), custom_call_target="tpu_custom_call" | custom-call | flops 10737418240 | bytes 12582912 | tf_op jit(solution)/shard_map/eliminate/pallas_call | solution.py:208
  (10 shorter events, 0.0 us)
Async XLA Ops:
  6.5 5.5 %copy-start.1 = (bf16[1,16,32,1024]{3,2,1,0:T(8,128)(2,1)S(1)}, bf16[1,16,32,1024]{3,2,1,0:T(8,128)(2,1)}, u32[]{:S(2)}) copy-start(bf16[1,16,32,1024]{3,2,1,0:T(8,128)(2,1)} %param.4) | copy-start | bytes 3145732
  6.5 112.6 %all-gather.2.cloned.1.call-start = ((), (), s32[]{:S(2)}) async-start(), calls=%async_computation.2 | async-start | bytes 4325376 | tf_op jit(solution)/shard_map/all_gather | solution.py:237
  14.4 39.4 %all-to-all-start = ((bf16[16,2,32,640]{3,2,1,0:T(8,128)(2,1)}), bf16[16,2,32,640]{3,2,1,0:T(8,128)(2,1)S(1)}, u32[]{:S(2)}, u32[]{:S(2)}) async-start(bf16[16,2,32,640]{3,2,1,0:T(8,128)(2,1)} %broadcast_select_fusion), calls=%async_computation | async-start | bytes 2621440 | tf_op jit(solution)/shard_map/all_to_all | solution.py:246
  54.1 65.0 %copy-start = (f32[1,2,1024,128]{3,2,1,0:T(8,128)S(1)}, f32[1,2,1024,128]{3,2,1,0:T(8,128)}, u32[]{:S(2)}) copy-start(f32[1,2,1024,128]{3,2,1,0:T(8,128)} %param.6) | copy-start | bytes 3145732
  89.9 21.3 %collective-permute-start.2 = (bf16[8,2,32,640]{3,2,1,0:T(8,128)(2,1)S(1)}, bf16[8,2,32,640]{3,2,1,0:T(8,128)(2,1)S(1)}, u32[]{:S(2)}, u32[]{:S(2)}) collective-permute-start(bf16[8,2,32,640]{3,2,1,0:T(8,128)(2,1)S(1)} %all_to_all.10.refs_0_), channel_id=1, source_target_pairs={{24,0},{25,1},{26,2},{27,3},{28,4},{29,5},{30,6},{31,7},{0,8},{1,9... | collective-permute-start | bytes 1966088 | tf_op jit(solution)/shard_map/ppermute | solution.py:28
  92.3 24.1 %collective-permute-start = (bf16[8,2,32,640]{3,2,1,0:T(8,128)(2,1)S(1)}, bf16[8,2,32,640]{3,2,1,0:T(8,128)(2,1)S(1)}, u32[]{:S(2)}, u32[]{:S(2)}) collective-permute-start(bf16[8,2,32,640]{3,2,1,0:T(8,128)(2,1)S(1)} %all_to_all.10.refs_0_), channel_id=1, source_target_pairs={{8,0},{9,1},{10,2},{11,3},{12,4},{13,5},{14,6},{15,7},{16,8},{17,9... | collective-permute-start | bytes 1966088 | tf_op jit(solution)/shard_map/ppermute | solution.py:28
  112.0 11.6 %collective-permute-start.3 = (bf16[4,2,32,640]{3,2,1,0:T(8,128)(2,1)}, bf16[4,2,32,640]{3,2,1,0:T(8,128)(2,1)S(1)}, u32[]{:S(2)}, u32[]{:S(2)}) collective-permute-start(bf16[4,2,32,640]{3,2,1,0:T(8,128)(2,1)} %slice.23), channel_id=1, source_target_pairs={{24,0},{25,1},{26,2},{27,3},{28,4},{29,5},{30,6},{31,7},{0,8},{1,9... | collective-permute-start | bytes 983048 | tf_op jit(solution)/shard_map/ppermute | solution.py:28
  117.1 12.5 %collective-permute-start.1 = (bf16[4,2,32,640]{3,2,1,0:T(8,128)(2,1)}, bf16[4,2,32,640]{3,2,1,0:T(8,128)(2,1)}, u32[]{:S(2)}, u32[]{:S(2)}) collective-permute-start(bf16[4,2,32,640]{3,2,1,0:T(8,128)(2,1)} %slice.22), channel_id=1, source_target_pairs={{8,0},{9,1},{10,2},{11,3},{12,4},{13,5},{14,6},{15,7},{16,8},{17,9... | collective-permute-start | bytes 983048 | tf_op jit(solution)/shard_map/ppermute | solution.py:28
Sparse Core Ops, SparseCore 0:
  10.5 98.7 all-gather.1

commit v3 on v2

--- a/solution.py
+++ b/solution.py
@@ -85,34 +85,53 @@
     lane = lax.broadcasted_iota(jnp.int32, (SUB, TILE), 1)
     upper_half = lax.broadcasted_iota(jnp.int32, (SUB, TILE), 0) < SUB // 2
     n_sub = TILE // SUB
-    tiles = [[work[slot, SUB * i : SUB * (i + 1), :] for i in range(n_sub)] for slot in range(2)]
+    tiles, scales = [], []
+    diagonal = lax.broadcasted_iota(jnp.int32, (TILE, TILE), 0) == lax.broadcasted_iota(jnp.int32, (TILE, TILE), 1)
+    for slot in range(2):
+        matrix = work[slot]
+        pivots = jnp.where(diagonal, matrix, 0.0)
+        scale = lax.rsqrt(jnp.sum(pivots, axis=0, keepdims=True))
+        matrix = matrix * lax.rsqrt(jnp.sum(pivots, axis=1, keepdims=True)) * scale
+        tiles.append([matrix[SUB * i : SUB * (i + 1), :] for i in range(n_sub)])
+        scales.append(jnp.broadcast_to(scale, (SUB, TILE)))
+    scale = jnp.where(upper_half, scales[0], scales[1])
     for s in range(n_sub):
         first = SUB * s
         inside = (lane >= first) & (lane < first + SUB)
+        done = jnp.where(lane < first + SUB, scale, 0.0)
         rows = [jnp.where(upper_half, row_of(tiles[0][s], r), row_of(tiles[1][s], r)) for r in range(SUB)]
         entry = [[lane_of(rows[r], first + c) for c in range(r + 1)] for r in range(SUB)]
         rows = [jnp.where(inside, jnp.where(lane == first + r, 1.0, 0.0), rows[r]) for r in range(SUB)]
-        ratio = [[None] * SUB for _ in range(SUB)]
-        inverse_pivot = [None] * SUB
-        for k in range(SUB):
-            inverse_pivot[k] = pl.reciprocal(entry[k][k], approx=True)
-            for r in range(k + 1, SUB):
-                ratio[r][k] = entry[r][k] * inverse_pivot[k]
-            for r in range(k + 1, SUB):
-                for c in range(k + 1, r + 1):
-                    entry[r][c] = entry[r][c] - ratio[r][k] * entry[c][k]
-                rows[r] = rows[r] - ratio[r][k] * rows[k]
         solved = [None] * SUB
-        for k in reversed(range(SUB)):
-            value = rows[k] * inverse_pivot[k]
-            for r in reversed(range(k + 1, SUB)):
-                value = value - ratio[r][k] * solved[r]
-            solved[k] = value
-        for k in range(SUB):
-            scaled = jnp.where(lane < first + SUB, rows[k] * lax.rsqrt(entry[k][k]), 0.0)
+        above = [None] * SUB
+        for p in range(0, SUB, 2):
+            q = p + 1
+            a, b, c = entry[p][p], entry[q][p], entry[q][q]
+            r = pl.reciprocal(a * c - b * b, approx=True)
+            ratio_p, ratio_q = [None] * SUB, [None] * SUB
+            for t in range(q + 1, SUB):
+                ratio_p[t] = (entry[t][p] * c - entry[t][q] * b) * r
+                ratio_q[t] = (entry[t][q] * a - entry[t][p] * b) * r
+            for t in range(q + 1, SUB):
+                for u in range(q + 1, t + 1):
+                    entry[t][u] = entry[t][u] - (ratio_p[t] * entry[u][p] + ratio_q[t] * entry[u][q])
+            root = lax.rsqrt(a)
+            lower = b * (root * root)
+            second = rows[q] - lower * rows[p]
+            finished = (rows[p] * root * done, second * lax.rsqrt(c - b * lower) * done)
             for slot in range(2):
                 at = slot * (SUB // 2)
-                inverse[slot, first + k : first + k + 1, :] = scaled[at : at + 1, :]
+                for k in range(2):
+                    inverse[slot, first + p + k : first + p + k + 1, :] = finished[k][at : at + 1, :]
+            solved[p] = rows[p] * (c * r) - rows[q] * (b * r)
+            solved[q] = rows[q] * (a * r) - rows[p] * (b * r)
+            for t in range(q + 1, SUB):
+                rows[t] = rows[t] - (ratio_p[t] * rows[p] + ratio_q[t] * rows[q])
+            for t in range(p):
+                solved[t] = solved[t] - (above[t][p] * solved[p] + above[t][q] * solved[q])
+                for u in range(q + 1, SUB):
+                    above[t][u] = above[t][u] - (above[t][p] * ratio_p[u] + above[t][q] * ratio_q[u])
+            above[p], above[q] = ratio_p, ratio_q
         if s + 1 == n_sub:
             break
         for slot in range(2):
@@ -228,25 +247,29 @@
     slab_rows, order = partial_stats.shape[2:]
     n_rows = slot_block.shape[0]
     group = lax.axis_index("group")
-    own_slots = lax.dynamic_index_in_dim(slot_block, lax.axis_index("dp"), 0, keepdims=False)
-    live = (own_slots >= 0)[:, None, None]
-    row = lax.broadcasted_iota(jnp.int32, (slab_rows, order), 0) + group * slab_rows
-    column = lax.broadcasted_iota(jnp.int32, (slab_rows, order), 1)
-
-    previous = jnp.where(live, old_basis[0], (row == column).astype(BF16)[None])
-    basis = lax.all_gather(previous, "group", axis=0)
+
+    basis = lax.all_gather(old_basis[0], "group", axis=0)
     back = back_moments(basis, exp_avg[0])
 
     kept = order // 2 + TILE
     block_start = group * slab_rows // TILE * TILE
     stats = jnp.concatenate([partial_stats[0], partial_stats[0, :, :, : kept - TILE]], axis=2)
     stats = lax.dynamic_slice_in_dim(stats, block_start, kept, axis=2)
-    sent = jnp.take(stats, jnp.maximum(slot_block.reshape(-1), 0), axis=0)
-    sent = sent.reshape(n_rows, 2, slab_rows, kept)
-    shares = lax.all_to_all(sent, "dp", split_axis=0, concat_axis=0)
-    identity = (row[:, :kept] == column[:, :kept] + block_start).astype(F32)[None]
-    factor = jnp.where(live, jnp.sum(shares.astype(F32), axis=0), identity).astype(BF16)
-
+
+    core = lax.rem(lax.axis_index("dp"), 2)
+    blocks = jnp.maximum(slot_block, 0).reshape(n_rows // 2, 2, 2)
+
+    def shares_for(core):
+        wanted = lax.dynamic_index_in_dim(blocks, core, 1, keepdims=False).reshape(-1)
+        return jnp.take(stats, wanted, axis=0, mode="clip").reshape(n_rows // 2, 2, slab_rows, kept)
+
+    other = lax.ppermute(shares_for(1 - core), "dp", [(d, d ^ 1) for d in range(n_rows)])
+    pairs = (shares_for(core).astype(F32) + other.astype(F32)).astype(BF16)
+    same_core = [list(range(c, n_rows, 2)) for c in range(2)]
+    shares = lax.all_to_all(pairs, "dp", split_axis=0, concat_axis=0, axis_index_groups=same_core)
+    factor = jnp.sum(shares.astype(F32), axis=0).astype(BF16)
+
+    own_slots = lax.dynamic_index_in_dim(slot_block, lax.axis_index("dp"), 0, keepdims=False)
     place = jnp.stack([group // Z_CHIPS, group % Z_CHIPS]).astype(jnp.int32)
     return eliminate(own_slots, place, gather_factor(factor), basis, back)[None]
 

time: 198 us -> 188 us (0.949)
  waiting for transfers between devices: 54.7 us -> 33 us
  blocking collectives: 35.8 us -> 57.1 us
  starting transfers between devices: 19.3 us -> 13.6 us
  other arithmetic: 5.07 us -> 1.32 us
    all_to_all x1 -> x0, waiting for transfers between devices: 32.1 us -> none  [on_device(): shares = lax.all_to_all(sent, 'dp', split_axis=0, concat_axis=0)]
    all_to_all x0 -> x1, blocking collectives: none -> 27.5 us  [on_device(): lax.all_to_all(pairs, 'dp', split_axis=0, concat_axis=0, axis_index_group...]
    ppermute x4, waiting for transfers between devices: 22.5 us -> 30.4 us  [from_neighbour(): return lax.ppermute(value, 'group', pairs)]
    all_to_all x1 -> x0, starting transfers between devices: 7.21 us -> none  [on_device(): shares = lax.all_to_all(sent, 'dp', split_axis=0, concat_axis=0)]
    all_to_all x1, blocking collectives: 35.8 us -> 29.6 us  [gather_factor(): lax.all_to_all(copies, 'group', split_axis=0, concat_axis=0, axis_index_g...]
    select_n x2 -> x0, other arithmetic: 2.9 us -> none  [the longest x1 1.64 us: on_device(): previous = jnp.where(live, old_basis[0], (row == column).astype(BF16)[None])]
  transfers between devices with their start and end apart: 6 -> 6, of which waited for: 4 -> 4; matrix products, arithmetic and copies ran while one was open for 4% -> 3% of each run, Pallas kernels for 2% -> 2%
where the time goes in v3:
time: 188 us
  Pallas kernels  64.4 us (34%)
  blocking collectives  57.1 us (30%)
  waiting for transfers between devices  33 us (18%)
  starting transfers between devices  13.6 us (7%)
  between operations  13.6 us (7%)
  local copies, waits for them, and re-layouts  4.78 us (3%)
    pallas_call x1, Pallas kernels, eliminate(): pl.pallas_call(eliminate_kernel, out_shape=jax.ShapeDtypeStruct((2, order...  61 us
    ppermute x4, waiting for transfers between devices, from_neighbour(): return lax.ppermute(value, 'group', pairs)  30.4 us
    all_to_all x1, blocking collectives, gather_factor(): lax.all_to_all(copies, 'group', split_axis=0, concat_axis=0, axis_index_g...  29.6 us
    all_to_all x1, blocking collectives, on_device(): lax.all_to_all(pairs, 'dp', split_axis=0, concat_axis=0, axis_index_group...  27.5 us
    ppermute x4, starting transfers between devices, from_neighbour(): return lax.ppermute(value, 'group', pairs)  11.7 us
  transfers between devices with their start and end apart: 6, of which 4 were waited for; matrix products, arithmetic and copies ran while one was open for 3% of the time, Pallas kernels for 2%

profile of v3, /device:TPU:6, one launch (start us, length us, event | category | flops | bytes accessed | tf_op | source)
XLA Modules:
  0.0 187.9 jit_solution(3721248995133579215)
XLA Ops:
  6.5 0.7 all-gather.2.cloned.1.call-update
  7.3 0.7 broadcast_maximum_fusion
  8.0 0.1 reshape.16
  8.0 0.1 constant_dynamic-slice_fusion
  8.1 0.1 copy.10
  8.3 0.1 reshape.29
  8.4 1.1 slice_bitcast_fusion
  9.4 0.3 fusion.1
  9.7 0.7 gather_fusion.1
  10.4 1.9 %collective-permute-start = (bf16[8,2,32,640]{3,2,1,0:T(8,128)(2,1)S(1)}, bf16[8,2,32,640]{3,2,1,0:T(8,128)(2,1)S(1)}, u32[]{:S(2)}, u32[]{:S(2)}) collective-permute-start(bf16[8,2,32,640]{3,2,1,0:T(8,128)(2,1)S(1)} %bitcast.19), channel_id=1, source_target_pairs={{0,32},{32,0},{64,96},{96,64},{128,160},{160,128},{192,224},{224,1... | collective-permute-start | bytes 1966088 | tf_op jit(solution)/shard_map/ppermute | solution.py:266
  12.3 0.1 copy.9
  12.5 0.1 reshape.21
  12.6 0.7 gather_fusion
  13.2 1.2 collective-permute-done
  14.4 0.2 fusion
  14.6 27.5 %all_to_all.10 = bf16[8,2,32,640]{3,2,1,0:T(8,128)(2,1)S(1)} all-to-all(bf16[8,2,32,640]{3,2,1,0:T(8,128)(2,1)S(1)} %fusion), channel_id=1, replica_groups={{0,64,128,192,256,320,384,448},{32,96,160,224,288,352,416,480},{1,65,12..., dimensions={0} | all-to-all | bytes 1310720 | tf_op jit(solution)/shard_map/all_to_all | solution.py:269
  42.1 0.1 reduce_sum.12
  42.2 0.1 broadcast_in_dim.18
  42.3 29.6 %all_to_all.11.refs_0_ = bf16[8,2,32,640]{3,2,1,0:T(8,128)(2,1)S(1)} all-to-all(bf16[8,2,32,640]{3,2,1,0:T(8,128)(2,1)S(1)} %broadcast_in_dim.18), channel_id=1, replica_groups={{0,1,2,3,4,5,6,7},{8,9,10,11,12,13,14,15},{16,17,18,19,20,21,22,23},{24..., dimensions={0} | all-to-all | bytes 1310720 | tf_op jit(solution)/shard_map/all_to_all | solution.py:34
  71.9 2.5 %collective-permute-start.3 = (bf16[8,2,32,640]{3,2,1,0:T(8,128)(2,1)S(1)}, bf16[8,2,32,640]{3,2,1,0:T(8,128)(2,1)S(1)}, u32[]{:S(2)}, u32[]{:S(2)}) collective-permute-start(bf16[8,2,32,640]{3,2,1,0:T(8,128)(2,1)S(1)} %all_to_all.11.refs_0_), channel_id=1, source_target_pairs={{24,0},{25,1},{26,2},{27,3},{28,4},{29,5},{30,6},{31,7},{0,8},{1,9... | collective-permute-start | bytes 1966088 | tf_op jit(solution)/shard_map/ppermute | solution.py:28
  74.4 3.3 %collective-permute-start.1 = (bf16[8,2,32,640]{3,2,1,0:T(8,128)(2,1)S(1)}, bf16[8,2,32,640]{3,2,1,0:T(8,128)(2,1)S(1)}, u32[]{:S(2)}, u32[]{:S(2)}) collective-permute-start(bf16[8,2,32,640]{3,2,1,0:T(8,128)(2,1)S(1)} %all_to_all.11.refs_0_), channel_id=1, source_target_pairs={{8,0},{9,1},{10,2},{11,3},{12,4},{13,5},{14,6},{15,7},{16,8},{17,9... | collective-permute-start | bytes 1966088 | tf_op jit(solution)/shard_map/ppermute | solution.py:28
  77.7 26.4 %collective-permute-done.3.refs_4_ = bf16[8,2,32,640]{3,2,1,0:T(8,128)(2,1)S(1)} collective-permute-done((bf16[8,2,32,640]{3,2,1,0:T(8,128)(2,1)S(1)}, bf16[8,2,32,640]{3,2,1,0:T(8,128)(2,1)S(1)}, u32[]{:S(2)}, u32[]{:S(2)}) %collective-permute-start.3) | collective-permute-done | bytes 655392 | tf_op jit(solution)/shard_map/ppermute | solution.py:28
  104.1 0.8 slice.17
  104.9 4.0 %collective-permute-start.4 = (bf16[4,2,32,640]{3,2,1,0:T(8,128)(2,1)}, bf16[4,2,32,640]{3,2,1,0:T(8,128)(2,1)S(1)}, u32[]{:S(2)}, u32[]{:S(2)}) collective-permute-start(bf16[4,2,32,640]{3,2,1,0:T(8,128)(2,1)} %slice.17), channel_id=1, source_target_pairs={{24,0},{25,1},{26,2},{27,3},{28,4},{29,5},{30,6},{31,7},{0,8},{1,9... | collective-permute-start | bytes 983048 | tf_op jit(solution)/shard_map/ppermute | solution.py:28
  108.8 0.8 slice.16
  109.6 1.9 %collective-permute-start.2 = (bf16[4,2,32,640]{3,2,1,0:T(8,128)(2,1)}, bf16[4,2,32,640]{3,2,1,0:T(8,128)(2,1)}, u32[]{:S(2)}, u32[]{:S(2)}) collective-permute-start(bf16[4,2,32,640]{3,2,1,0:T(8,128)(2,1)} %slice.16), channel_id=1, source_target_pairs={{8,0},{9,1},{10,2},{11,3},{12,4},{13,5},{14,6},{15,7},{16,8},{17,9... | collective-permute-start | bytes 983048 | tf_op jit(solution)/shard_map/ppermute | solution.py:28
  111.5 0.2 fusion.2.live
  111.7 0.1 pad_add_fusion.place
  111.8 0.8 all-gather.2.cloned.1.call-done.basis.refs_5_
  112.6 3.4 %back_moments.1.refs_6_ = bf16[2,1024,256]{2,1,0:T(8,128)(2,1)S(1)} custom-call(bf16[32,2,32,1024]{3,2,1,0:T(8,128)(2,1)} %all-gather.2.cloned.1.call-done.basis.refs_5_, f32[2,1024,128]{2,1,0:T(8,128)S(1)} %bitcast.16), custom_call_target="tpu_custom_call" | custom-call | flops 1073741824 | bytes 6291456 | tf_op jit(solution)/shard_map/back_moments/pallas_call | solution.py:213
  116.1 4.0 %collective-permute-done.2.refs_2_ = bf16[4,2,32,640]{3,2,1,0:T(8,128)(2,1)} collective-permute-done((bf16[4,2,32,640]{3,2,1,0:T(8,128)(2,1)}, bf16[4,2,32,640]{3,2,1,0:T(8,128)(2,1)}, u32[]{:S(2)}, u32[]{:S(2)}) %collective-permute-start.2) | collective-permute-done | bytes 327712 | tf_op jit(solution)/shard_map/ppermute | solution.py:28
  120.1 61.0 %eliminate.1 = f32[2,1024,128]{2,1,0:T(8,128)} custom-call(s32[2]{0:T(128)S(1)} %fusion.2.live, s32[2]{0:T(128)S(1)} %pad_add_fusion.place, bf16[8,2,32,640]{3,2,1,0:T(8,128)(2,1)S(1)} %all_to_all.11.refs_0_, bf16[8,2,32,640]{3,2,1,0:T(8,128)(2,1)S(1)} %collective-permute-done.1.refs_1_, bf16[4,2,32,640]{3,2,1,0:T(8,128)(2,1)} %collective-permute-done.2.refs_2_, ...), custom_call_target="tpu_custom_call" | custom-call | flops 10737418240 | bytes 12582912 | tf_op jit(solution)/shard_map/eliminate/pallas_call | solution.py:227
  (11 shorter events, 0.0 us)
Async XLA Ops:
  6.5 2.9 %copy-start.1 = (bf16[1,16,32,1024]{3,2,1,0:T(8,128)(2,1)S(1)}, bf16[1,16,32,1024]{3,2,1,0:T(8,128)(2,1)}, u32[]{:S(2)}) copy-start(bf16[1,16,32,1024]{3,2,1,0:T(8,128)(2,1)} %param.4) | copy-start | bytes 3145732
  6.5 106.1 %all-gather.2.cloned.1.call-start = ((), (), s32[]{:S(2)}) async-start(), calls=%async_computation.2 | async-start | bytes 4325376 | tf_op jit(solution)/shard_map/all_gather | solution.py:251
  10.4 4.0 %collective-permute-start = (bf16[8,2,32,640]{3,2,1,0:T(8,128)(2,1)S(1)}, bf16[8,2,32,640]{3,2,1,0:T(8,128)(2,1)S(1)}, u32[]{:S(2)}, u32[]{:S(2)}) collective-permute-start(bf16[8,2,32,640]{3,2,1,0:T(8,128)(2,1)S(1)} %bitcast.19), channel_id=1, source_target_pairs={{0,32},{32,0},{64,96},{96,64},{128,160},{160,128},{192,224},{224,1... | collective-permute-start | bytes 1966088 | tf_op jit(solution)/shard_map/ppermute | solution.py:266
  42.2 69.3 %copy-start.2 = (s32[16,2]{0,1:T(2,128)S(1)}, s32[16,2]{0,1:T(2,128)}, u32[]{:S(2)}) copy-start(s32[16,2]{0,1:T(2,128)} %param.7) | copy-start | bytes 388
  42.3 70.4 %copy-start = (f32[1,2,1024,128]{3,2,1,0:T(8,128)S(1)}, f32[1,2,1024,128]{3,2,1,0:T(8,128)}, u32[]{:S(2)}) copy-start(f32[1,2,1024,128]{3,2,1,0:T(8,128)} %param.6) | copy-start | bytes 3145732
  71.9 32.2 %collective-permute-start.3 = (bf16[8,2,32,640]{3,2,1,0:T(8,128)(2,1)S(1)}, bf16[8,2,32,640]{3,2,1,0:T(8,128)(2,1)S(1)}, u32[]{:S(2)}, u32[]{:S(2)}) collective-permute-start(bf16[8,2,32,640]{3,2,1,0:T(8,128)(2,1)S(1)} %all_to_all.11.refs_0_), channel_id=1, source_target_pairs={{24,0},{25,1},{26,2},{27,3},{28,4},{29,5},{30,6},{31,7},{0,8},{1,9... | collective-permute-start | bytes 1966088 | tf_op jit(solution)/shard_map/ppermute | solution.py:28
  74.4 34.4 %collective-permute-start.1 = (bf16[8,2,32,640]{3,2,1,0:T(8,128)(2,1)S(1)}, bf16[8,2,32,640]{3,2,1,0:T(8,128)(2,1)S(1)}, u32[]{:S(2)}, u32[]{:S(2)}) collective-permute-start(bf16[8,2,32,640]{3,2,1,0:T(8,128)(2,1)S(1)} %all_to_all.11.refs_0_), channel_id=1, source_target_pairs={{8,0},{9,1},{10,2},{11,3},{12,4},{13,5},{14,6},{15,7},{16,8},{17,9... | collective-permute-start | bytes 1966088 | tf_op jit(solution)/shard_map/ppermute | solution.py:28
  104.9 11.2 %collective-permute-start.4 = (bf16[4,2,32,640]{3,2,1,0:T(8,128)(2,1)}, bf16[4,2,32,640]{3,2,1,0:T(8,128)(2,1)S(1)}, u32[]{:S(2)}, u32[]{:S(2)}) collective-permute-start(bf16[4,2,32,640]{3,2,1,0:T(8,128)(2,1)} %slice.17), channel_id=1, source_target_pairs={{24,0},{25,1},{26,2},{27,3},{28,4},{29,5},{30,6},{31,7},{0,8},{1,9... | collective-permute-start | bytes 983048 | tf_op jit(solution)/shard_map/ppermute | solution.py:28
  109.6 10.5 %collective-permute-start.2 = (bf16[4,2,32,640]{3,2,1,0:T(8,128)(2,1)}, bf16[4,2,32,640]{3,2,1,0:T(8,128)(2,1)}, u32[]{:S(2)}, u32[]{:S(2)}) collective-permute-start(bf16[4,2,32,640]{3,2,1,0:T(8,128)(2,1)} %slice.16), channel_id=1, source_target_pairs={{8,0},{9,1},{10,2},{11,3},{12,4},{13,5},{14,6},{15,7},{16,8},{17,9... | collective-permute-start | bytes 983048 | tf_op jit(solution)/shard_map/ppermute | solution.py:28
Sparse Core Ops, SparseCore 0:
  10.5 102.0 all-gather.1

commit v4 on v3

v4 whole, which is shorter than its diff:
```python
import functools

import jax
import jax.numpy as jnp
from jax import lax
from jax.experimental import pallas as pl
from jax.experimental.pallas import tpu as pltpu
from jax.sharding import PartitionSpec as P

BF16, F32 = jnp.bfloat16, jnp.float32
VMEM_BYTES = 48 * 1024 * 1024
TILE = 128
SUB = 8
PANEL = 32
X_CHIPS, Z_CHIPS = 4, 8
ALONG_Z = [[x * Z_CHIPS + z for z in range(Z_CHIPS)] for x in range(X_CHIPS)]
ALONG_X = [[x * Z_CHIPS + z for x in range(X_CHIPS)] for z in range(Z_CHIPS)]


def high_low(value):
    high = value.astype(BF16)
    return high, (value - high.astype(F32)).astype(BF16)


def from_neighbour(value, dx, dz):
    pairs = []
    for x in range(X_CHIPS):
        for z in range(Z_CHIPS):
            source = (x + dx) % X_CHIPS * Z_CHIPS + (z + dz) % Z_CHIPS
            pairs.append((source, x * Z_CHIPS + z))
    return lax.ppermute(value, "group", pairs)


def gather_factor(slab):
    copies = jnp.broadcast_to(slab[None], (Z_CHIPS,) + slab.shape)
    own = lax.all_to_all(copies, "group", split_axis=0, concat_axis=0, axis_index_groups=ALONG_Z)
    after = from_neighbour(own, 1, 0)
    before = from_neighbour(own, -1, 0)
    half = Z_CHIPS // 2
    across_low = from_neighbour(after[:half], 1, 0)
    across_high = from_neighbour(before[half:], -1, 0)
    return own, after, across_low, across_high, before


def fill_factor(x, pieces, factor):
    own, after, across_low, across_high, before = pieces
    half = Z_CHIPS // 2
    blocks = factor.shape[1] // TILE
    for distance in range(X_CHIPS):
        for z_half in range(2):
            block_row = lax.rem(x + distance, X_CHIPS) * 2 + z_half
            here = pl.ds(pl.multiple_of(block_row * TILE, TILE), TILE)
            for slot in range(2):
                if distance == 2:
                    piece = (across_low, across_high)[z_half][:, slot]
                else:
                    piece = (own, after, None, before)[distance][half * z_half : half * (z_half + 1), slot]
                piece = piece.reshape(TILE, piece.shape[2])
                for k in range(blocks // 2 + 1):
                    there = pl.ds(pl.multiple_of(lax.rem(block_row + k, blocks) * TILE, TILE), TILE)
                    block = piece[:, TILE * k : TILE * (k + 1)]
                    factor[slot, here, there] = block
                    if 0 < k < blocks // 2:
                        factor[slot, there, here] = block.T


def row_of(value, at):
    return jnp.broadcast_to(value[at : at + 1, :], value.shape)


def lane_of(value, at):
    return jnp.broadcast_to(value[:, at : at + 1], value.shape)


def inverse_factors(work, done, inverse):
    lane = lax.broadcasted_iota(jnp.int32, (SUB, TILE), 1)
    upper_half = lax.broadcasted_iota(jnp.int32, (SUB, TILE), 0) < SUB // 2
    whole_row = lax.broadcasted_iota(jnp.int32, (TILE, TILE), 0)
    whole_lane = lax.broadcasted_iota(jnp.int32, (TILE, TILE), 1)
    scales = []
    for slot in range(2):
        matrix = work[slot]
        pivots = jnp.where(whole_row == whole_lane, matrix, 0.0)
        scale = lax.rsqrt(jnp.sum(pivots, axis=0, keepdims=True))
        work[slot] = matrix * lax.rsqrt(jnp.sum(pivots, axis=1, keepdims=True)) * scale
        scales.append(scale)
    for panel in range(0, TILE, PANEL):
        n_sub = PANEL // SUB
        tiles = [[work[slot, panel + SUB * i : panel + SUB * (i + 1), :] for i in range(n_sub)] for slot in range(2)]
        for s in range(n_sub):
            eliminate_rows(tiles, s, panel + SUB * s, lane, upper_half, done)
        end = panel + PANEL
        if end == TILE:
            break
        row = whole_row[:PANEL] + panel
        inner = whole_lane[:PANEL] < end
        below = whole_lane[: TILE - end]
        for slot in range(2):
            rows = done[slot, panel:end, :]
            rows = jnp.where(inner & (whole_lane[:PANEL] > row), 0.0, rows)
            high, low = high_low(rows)
            left = jnp.concatenate([high, high, low], axis=0).astype(F32).T[end:, :].astype(BF16)
            product = jnp.dot(left, jnp.concatenate([high, low, high], axis=0), preferred_element_type=F32)
            old = jnp.where((below >= panel) & (below < end), 0.0, work[slot, end:, :])
            work[slot, end:, :] = old - product
    for slot in range(2):
        inverse[slot] = jnp.where(whole_lane <= whole_row, done[slot] * scales[slot], 0.0)


def eliminate_rows(tiles, s, first, lane, upper_half, done):
    inside = (lane >= first) & (lane < first + SUB)
    rows = [jnp.where(upper_half, row_of(tiles[0][s], r), row_of(tiles[1][s], r)) for r in range(SUB)]
    entry = [[lane_of(rows[r], first + c) for c in range(r + 1)] for r in range(SUB)]
    rows = [jnp.where(inside, jnp.where(lane == first + r, 1.0, 0.0), rows[r]) for r in range(SUB)]
    more = s + 1 < len(tiles[0])
    solved = [None] * SUB
    above = [None] * SUB
    for p in range(0, SUB, 2):
        q = p + 1
        a, b, c = entry[p][p], entry[q][p], entry[q][q]
        r = pl.reciprocal(a * c - b * b, approx=True)
        ratio_p, ratio_q = [None] * SUB, [None] * SUB
        for t in range(q + 1, SUB):
            ratio_p[t] = (entry[t][p] * c - entry[t][q] * b) * r
            ratio_q[t] = (entry[t][q] * a - entry[t][p] * b) * r
        for t in range(q + 1, SUB):
            for u in range(q + 1, t + 1):
                entry[t][u] = entry[t][u] - (ratio_p[t] * entry[u][p] + ratio_q[t] * entry[u][q])
        root = lax.rsqrt(a)
        lower = b * (root * root)
        finished = (rows[p] * root, (rows[q] - lower * rows[p]) * lax.rsqrt(c - b * lower))
        for slot in range(2):
            at = slot * (SUB // 2)
            for k in range(2):
                done[slot, first + p + k : first + p + k + 1, :] = finished[k][at : at + 1, :]
        for t in range(q + 1, SUB):
            rows[t] = rows[t] - (ratio_p[t] * rows[p] + ratio_q[t] * rows[q])
        if not more:
            continue
        solved[p] = rows[p] * (c * r) - rows[q] * (b * r)
        solved[q] = rows[q] * (a * r) - rows[p] * (b * r)
        for t in range(p):
            solved[t] = solved[t] - (above[t][p] * solved[p] + above[t][q] * solved[q])
            for u in range(q + 1, SUB):
                above[t][u] = above[t][u] - (above[t][p] * ratio_p[u] + above[t][q] * ratio_q[u])
        above[p], above[q] = ratio_p, ratio_q
    if not more:
        return
    for slot in range(2):
        spread = [row_of(solved[k], slot * (SUB // 2)) for k in range(SUB)]
        for i in range(s + 1, len(tiles[slot])):
            old = tiles[slot][i]
            terms = [lane_of(old, first + c) * spread[c] for c in range(SUB)]
            while len(terms) > 1:
                terms = [a + b for a, b in zip(terms[::2], terms[1::2])]
            tiles[slot][i] = jnp.where(inside, 0.0, old) - terms[0]


def normal_equations(basis, moment, factor, projected, transposed, system):
    order = factor.shape[1]
    width = moment.shape[2]
    chunk = 2 * TILE
    for slot in range(2):
        for at in range(0, order, chunk):
            columns = basis[:, slot, :, at : at + chunk].reshape(order, chunk)
            product = jnp.dot(factor[slot], columns, preferred_element_type=F32).astype(BF16)
            projected[slot, :, at : at + chunk] = product
            transposed[slot, at : at + chunk, :] = product.T
        for at in range(0, order, chunk):
            end = at + chunk
            product = jnp.dot(transposed[slot, :end, :], projected[slot, :, at:end], preferred_element_type=F32)
            system[slot, : end // TILE, :, at:end] = product.reshape(end // TILE, TILE, chunk)
        product = moment[slot]
        for left in (basis[:, slot].reshape(order, order), transposed[slot]):
            product = jnp.dot(left, jnp.concatenate(high_low(product), axis=1), preferred_element_type=F32)
            product = product[:, :width] + product[:, width:]
        system[slot, :, :, order:] = product.reshape(order // TILE, TILE, width)


def finish_block(block, live, inverse, system, out):
    order = out.shape[1]
    first = TILE * (block + 1)
    below = order - first
    for slot in range(2):
        high, low = high_low(inverse[slot])
        left = jnp.concatenate([high, high, low], axis=1)
        high, low = high_low(system[slot, block, :, first:])
        right = jnp.concatenate([high, low, high], axis=0)
        solved = jnp.dot(left, right, preferred_element_type=F32)
        out[slot, first - TILE : first, :] = jnp.where(live[slot] >= 0, solved[:, below:], 0.0)
        if below == 0:
            continue
        high, low = high_low(solved)
        right = jnp.concatenate([high, low, high], axis=0)
        high, low = high_low(solved[:, :below].T)
        left = jnp.concatenate([high, high, low], axis=1)
        end = right.shape[1]
        while end > 0:
            start = max(end - 2 * TILE, 0)
            rows = min(end, below)
            product = jnp.dot(left[:rows], right[:, start:end], preferred_element_type=F32)
            product = product.reshape(rows // TILE, TILE, end - start)
            system[slot, block + 1 : block + 1 + rows // TILE, :, first + start : first + end] -= product
            end = start


def eliminate_kernel(live, place, *refs):
    pieces, basis, moment, out = refs[:5], refs[5], refs[6], refs[7]
    factor, projected, transposed, system, work, done, inverse = refs[8:]
    blocks = out.shape[1] // TILE
    fill_factor(place[0], pieces, factor)
    normal_equations(basis, moment, factor, projected, transposed, system)

    def step(j, carry):
        for slot in range(2):
            work[slot] = system[slot, j, :, pl.ds(pl.multiple_of(j * TILE, TILE), TILE)]
        inverse_factors(work, done, inverse)
        for block in range(blocks):
            pl.when(j == block)(functools.partial(finish_block, block, live, inverse, system, out))
        return carry

    lax.fori_loop(0, blocks, step, 0)


def eliminate(live, place, pieces, basis, moment):
    _, order, width = moment.shape
    smem = pl.BlockSpec(memory_space=pltpu.SMEM)
    vmem = pl.BlockSpec(memory_space=pltpu.VMEM)
    return pl.pallas_call(
        eliminate_kernel,
        out_shape=jax.ShapeDtypeStruct((2, order, width), F32),
        in_specs=[smem, smem] + [vmem] * 7,
        out_specs=vmem,
        scratch_shapes=[
            pltpu.VMEM((2, order, order), BF16),
            pltpu.VMEM((2, order, order), BF16),
            pltpu.VMEM((2, order, order), BF16),
            pltpu.VMEM((2, order // TILE, TILE, order + width), F32),
            pltpu.VMEM((2, TILE, TILE), F32),
            pltpu.VMEM((2, TILE, TILE), F32),
            pltpu.VMEM((2, TILE, TILE), F32),
        ],
        compiler_params=pltpu.CompilerParams(vmem_limit_bytes=VMEM_BYTES),
        cost_estimate=pl.CostEstimate(flops=10 * order**3, bytes_accessed=12 << 20, transcendentals=0),
        name="eliminate",
    )(live, place, *pieces, basis, moment)


def on_device(partial_stats, old_basis, exp_avg, slot_block):
    slab_rows, order = partial_stats.shape[2:]
    n_rows = slot_block.shape[0]
    group = lax.axis_index("group")

    basis = lax.all_gather(old_basis[0], "group", axis=0, axis_index_groups=ALONG_Z)

    kept = order // 2 + TILE
    block_start = group * slab_rows // TILE * TILE
    stats = jnp.concatenate([partial_stats[0], partial_stats[0, :, :, : kept - TILE]], axis=2)
    stats = lax.dynamic_slice_in_dim(stats, block_start, kept, axis=2)

    core = lax.rem(lax.axis_index("dp"), 2)
    blocks = jnp.maximum(slot_block, 0).reshape(n_rows // 2, 2, 2)

    def shares_for(core):
        wanted = lax.dynamic_index_in_dim(blocks, core, 1, keepdims=False).reshape(-1)
        return jnp.take(stats, wanted, axis=0, mode="clip").reshape(n_rows // 2, 2, slab_rows, kept)

    other = lax.ppermute(shares_for(1 - core), "dp", [(d, d ^ 1) for d in range(n_rows)])
    pairs = (shares_for(core).astype(F32) + other.astype(F32)).astype(BF16)
    same_core = [list(range(c, n_rows, 2)) for c in range(2)]
    shares = lax.all_to_all(pairs, "dp", split_axis=0, concat_axis=0, axis_index_groups=same_core)
    shares, basis = lax.optimization_barrier((shares, basis))
    basis = lax.all_gather(basis, "group", axis=0, axis_index_groups=ALONG_X)
    basis = basis.reshape((X_CHIPS * Z_CHIPS,) + basis.shape[2:])
    factor = jnp.sum(shares.astype(F32), axis=0).astype(BF16)

    own_slots = lax.dynamic_index_in_dim(slot_block, lax.axis_index("dp"), 0, keepdims=False)
    place = jnp.stack([group // Z_CHIPS, group % Z_CHIPS]).astype(jnp.int32)
    return eliminate(own_slots, place, gather_factor(factor), basis, exp_avg[0])[None]


def solution(mesh):
    return jax.shard_map(
        on_device,
        mesh=mesh,
        in_specs=(
            P("dp", None, "group", None),
            P("dp", None, "group", None),
            P("dp", None, None, "group"),
            P(),
        ),
        out_specs=P("dp", None, None, "group"),
        check_vma=False,
    )
```

time: 188 us -> 194 us (1.032); the launches traced: 188 us -> 191 us
  waiting for transfers between devices: 33 us -> 56.8 us
  Pallas kernels: 64.4 us -> 52.4 us
  blocking collectives: 57.1 us -> 48.2 us
    all_gather x1 -> x2, waiting for transfers between devices: 0.81 us -> 17.3 us  [the longest x1 17.2 us: on_device(): lax.all_gather(old_basis[0], 'group', axis=0, axis_index_groups=ALONG_Z)]
    all_to_all x1, blocking collectives: 29.6 us -> 20.7 us  [gather_factor(): lax.all_to_all(copies, 'group', split_axis=0, concat_axis=0, axis_index_g...]
    pallas_call x1, Pallas kernels: 61 us -> 52.4 us  [eliminate(): pl.pallas_call(eliminate_kernel, out_shape=jax.ShapeDtypeStruct((2, order...]
    ppermute x4, waiting for transfers between devices: 30.4 us -> 38.4 us  [from_neighbour(): return lax.ppermute(value, 'group', pairs)]
    pallas_call x1 -> x0, Pallas kernels: 3.45 us -> none  [back_moments(): pl.pallas_call(back_kernel, out_shape=jax.ShapeDtypeStruct((2, order, 2 *...]
  transfers between devices with their start and end apart: 6 -> 7, of which waited for: 4 -> 6; matrix products, arithmetic and copies ran while one was open for 3% -> 2% of each run, Pallas kernels for 2% -> 0%
where the time goes in v4:
time: 194 us; the launch traced here: 191 us
  waiting for transfers between devices  56.8 us (29%)
  Pallas kernels  52.4 us (27%)
  blocking collectives  48.2 us (25%)
  starting transfers between devices  13.6 us (7%)
  between operations  13.6 us (7%)
  local copies, waits for them, and re-layouts  4.78 us (2%)
    pallas_call x1, Pallas kernels, eliminate(): pl.pallas_call(eliminate_kernel, out_shape=jax.ShapeDtypeStruct((2, order...  52.4 us
    ppermute x4, waiting for transfers between devices, from_neighbour(): return lax.ppermute(value, 'group', pairs)  38.4 us
    all_to_all x1, blocking collectives, on_device(): lax.all_to_all(pairs, 'dp', split_axis=0, concat_axis=0, axis_index_group...  27.5 us
    all_to_all x1, blocking collectives, gather_factor(): lax.all_to_all(copies, 'group', split_axis=0, concat_axis=0, axis_index_g...  20.7 us
    all_gather x1, waiting for transfers between devices, on_device(): lax.all_gather(old_basis[0], 'group', axis=0, axis_index_groups=ALONG_Z)  17.2 us
    ppermute x4, starting transfers between devices, from_neighbour(): return lax.ppermute(value, 'group', pairs)  11.7 us
  transfers between devices with their start and end apart: 7, of which 6 were waited for; matrix products, arithmetic and copies ran while one was open for 2% of the time, Pallas kernels for 0%

profile of v4, /device:TPU:6, one launch (start us, length us, event | category | flops | bytes accessed | tf_op | source)
XLA Modules:
  0.0 190.7 jit_solution(10340038100343732122)
XLA Ops:
  6.5 0.8 broadcast_maximum_fusion
  7.3 0.1 reshape.19
  7.4 0.1 constant_dynamic-slice_fusion
  7.5 0.1 copy.10
  7.6 0.1 reshape.33
  7.7 1.1 slice_bitcast_fusion
  8.8 0.3 fusion.1
  9.1 0.7 gather_fusion.1
  9.8 1.9 %collective-permute-start = (bf16[8,2,32,640]{3,2,1,0:T(8,128)(2,1)S(1)}, bf16[8,2,32,640]{3,2,1,0:T(8,128)(2,1)S(1)}, u32[]{:S(2)}, u32[]{:S(2)}) collective-permute-start(bf16[8,2,32,640]{3,2,1,0:T(8,128)(2,1)S(1)} %bitcast.19), channel_id=1, source_target_pairs={{0,32},{32,0},{64,96},{96,64},{128,160},{160,128},{192,224},{224,1... | collective-permute-start | bytes 1966088 | tf_op jit(solution)/shard_map/ppermute | solution.py:268
  11.8 0.1 copy.9
  11.9 0.1 reshape.25
  12.0 0.7 gather_fusion
  12.7 1.1 collective-permute-done
  13.8 0.2 fusion
  13.9 27.5 %all_to_all.10 = bf16[8,2,32,640]{3,2,1,0:T(8,128)(2,1)S(1)} all-to-all(bf16[8,2,32,640]{3,2,1,0:T(8,128)(2,1)S(1)} %fusion), channel_id=1, replica_groups={{0,64,128,192,256,320,384,448},{32,96,160,224,288,352,416,480},{1,65,12..., dimensions={0} | all-to-all | bytes 1310720 | tf_op jit(solution)/shard_map/all_to_all | solution.py:271
  41.4 17.2 %all-gather.4.cloned.1.call-done = bf16[8,2,32,1024]{3,2,1,0:T(8,128)(2,1)} async-done(((bf16[1,2,32,1024]{3,2,1,0:T(8,128)(2,1)}), bf16[8,2,32,1024]{3,2,1,0:T(8,128)(2,1)}) %all-gather.4.cloned.1.call-update) | async-done | bytes 1048592 | tf_op jit(solution)/shard_map/all_gather | solution.py:254
  58.6 0.1 reduce_sum.12
  58.7 0.1 broadcast_in_dim.18
  58.8 20.7 %all_to_all.11.refs_0_ = bf16[8,2,32,640]{3,2,1,0:T(8,128)(2,1)S(1)} all-to-all(bf16[8,2,32,640]{3,2,1,0:T(8,128)(2,1)S(1)} %broadcast_in_dim.18), channel_id=1, replica_groups={{0,1,2,3,4,5,6,7},{8,9,10,11,12,13,14,15},{16,17,18,19,20,21,22,23},{24..., dimensions={0} | all-to-all | bytes 1310720 | tf_op jit(solution)/shard_map/all_to_all | solution.py:36
  79.5 2.4 %collective-permute-start.3 = (bf16[8,2,32,640]{3,2,1,0:T(8,128)(2,1)S(1)}, bf16[8,2,32,640]{3,2,1,0:T(8,128)(2,1)S(1)}, u32[]{:S(2)}, u32[]{:S(2)}) collective-permute-start(bf16[8,2,32,640]{3,2,1,0:T(8,128)(2,1)S(1)} %all_to_all.11.refs_0_), channel_id=1, source_target_pairs={{24,0},{25,1},{26,2},{27,3},{28,4},{29,5},{30,6},{31,7},{0,8},{1,9... | collective-permute-start | bytes 1966088 | tf_op jit(solution)/shard_map/ppermute | solution.py:31
  81.9 3.4 %collective-permute-start.1 = (bf16[8,2,32,640]{3,2,1,0:T(8,128)(2,1)S(1)}, bf16[8,2,32,640]{3,2,1,0:T(8,128)(2,1)S(1)}, u32[]{:S(2)}, u32[]{:S(2)}) collective-permute-start(bf16[8,2,32,640]{3,2,1,0:T(8,128)(2,1)S(1)} %all_to_all.11.refs_0_), channel_id=1, source_target_pairs={{8,0},{9,1},{10,2},{11,3},{12,4},{13,5},{14,6},{15,7},{16,8},{17,9... | collective-permute-start | bytes 1966088 | tf_op jit(solution)/shard_map/ppermute | solution.py:31
  85.3 25.8 %collective-permute-done.3.refs_4_ = bf16[8,2,32,640]{3,2,1,0:T(8,128)(2,1)S(1)} collective-permute-done((bf16[8,2,32,640]{3,2,1,0:T(8,128)(2,1)S(1)}, bf16[8,2,32,640]{3,2,1,0:T(8,128)(2,1)S(1)}, u32[]{:S(2)}, u32[]{:S(2)}) %collective-permute-start.3) | collective-permute-done | bytes 655392 | tf_op jit(solution)/shard_map/ppermute | solution.py:31
  111.1 0.8 slice.17
  111.8 3.3 %collective-permute-start.4 = (bf16[4,2,32,640]{3,2,1,0:T(8,128)(2,1)}, bf16[4,2,32,640]{3,2,1,0:T(8,128)(2,1)S(1)}, u32[]{:S(2)}, u32[]{:S(2)}) collective-permute-start(bf16[4,2,32,640]{3,2,1,0:T(8,128)(2,1)} %slice.17), channel_id=1, source_target_pairs={{24,0},{25,1},{26,2},{27,3},{28,4},{29,5},{30,6},{31,7},{0,8},{1,9... | collective-permute-start | bytes 983048 | tf_op jit(solution)/shard_map/ppermute | solution.py:31
  115.2 0.8 slice.16
  116.0 2.5 %collective-permute-start.2 = (bf16[4,2,32,640]{3,2,1,0:T(8,128)(2,1)}, bf16[4,2,32,640]{3,2,1,0:T(8,128)(2,1)}, u32[]{:S(2)}, u32[]{:S(2)}) collective-permute-start(bf16[4,2,32,640]{3,2,1,0:T(8,128)(2,1)} %slice.16), channel_id=1, source_target_pairs={{8,0},{9,1},{10,2},{11,3},{12,4},{13,5},{14,6},{15,7},{16,8},{17,9... | collective-permute-start | bytes 983048 | tf_op jit(solution)/shard_map/ppermute | solution.py:31
  118.5 0.2 fusion.2.live
  118.7 0.1 pad_add_fusion.place
  118.7 10.4 %collective-permute-done.4.refs_3_ = bf16[4,2,32,640]{3,2,1,0:T(8,128)(2,1)S(1)} collective-permute-done((bf16[4,2,32,640]{3,2,1,0:T(8,128)(2,1)}, bf16[4,2,32,640]{3,2,1,0:T(8,128)(2,1)S(1)}, u32[]{:S(2)}, u32[]{:S(2)}) %collective-permute-start.4) | collective-permute-done | bytes 327712 | tf_op jit(solution)/shard_map/ppermute | solution.py:31
  129.1 2.2 %collective-permute-done.2.refs_2_ = bf16[4,2,32,640]{3,2,1,0:T(8,128)(2,1)} collective-permute-done((bf16[4,2,32,640]{3,2,1,0:T(8,128)(2,1)}, bf16[4,2,32,640]{3,2,1,0:T(8,128)(2,1)}, u32[]{:S(2)}, u32[]{:S(2)}) %collective-permute-start.2) | collective-permute-done | bytes 327712 | tf_op jit(solution)/shard_map/ppermute | solution.py:31
  131.3 0.2 all-gather.6.cloned.1.call-done.refs_5_
  131.5 52.4 %eliminate.1 = f32[2,1024,128]{2,1,0:T(8,128)} custom-call(s32[2]{0:T(128)S(1)} %fusion.2.live, s32[2]{0:T(128)S(1)} %pad_add_fusion.place, bf16[8,2,32,640]{3,2,1,0:T(8,128)(2,1)S(1)} %all_to_all.11.refs_0_, bf16[8,2,32,640]{3,2,1,0:T(8,128)(2,1)S(1)} %collective-permute-done.1.refs_1_, bf16[4,2,32,640]{3,2,1,0:T(8,128)(2,1)} %collective-permute-done.2.refs_2_, ...), custom_call_target="tpu_custom_call" | custom-call | flops 10737418240 | bytes 12582912 | tf_op jit(solution)/shard_map/eliminate/pallas_call | solution.py:229
  (13 shorter events, 0.1 us)
Async XLA Ops:
  6.5 2.3 %copy-start.1 = (bf16[1,16,32,1024]{3,2,1,0:T(8,128)(2,1)S(1)}, bf16[1,16,32,1024]{3,2,1,0:T(8,128)(2,1)}, u32[]{:S(2)}) copy-start(bf16[1,16,32,1024]{3,2,1,0:T(8,128)(2,1)} %param.4) | copy-start | bytes 3145732
  6.5 52.1 %all-gather.4.cloned.1.call-start = ((), (), s32[]{:S(2)}) async-start(), calls=%async_computation.2 | async-start | bytes 1179648 | tf_op jit(solution)/shard_map/all_gather | solution.py:254
  9.8 4.0 %collective-permute-start = (bf16[8,2,32,640]{3,2,1,0:T(8,128)(2,1)S(1)}, bf16[8,2,32,640]{3,2,1,0:T(8,128)(2,1)S(1)}, u32[]{:S(2)}, u32[]{:S(2)}) collective-permute-start(bf16[8,2,32,640]{3,2,1,0:T(8,128)(2,1)S(1)} %bitcast.19), channel_id=1, source_target_pairs={{0,32},{32,0},{64,96},{96,64},{128,160},{160,128},{192,224},{224,1... | collective-permute-start | bytes 1966088 | tf_op jit(solution)/shard_map/ppermute | solution.py:268
  11.7 119.8 %all-gather.6.cloned.1.call-start = ((), (), s32[]{:S(2)}) async-start(), calls=%async_computation.3 | async-start | bytes 5242880 | tf_op jit(solution)/shard_map/all_gather | solution.py:273
  58.8 59.7 %copy-start.2 = (s32[16,2]{0,1:T(2,128)S(1)}, s32[16,2]{0,1:T(2,128)}, u32[]{:S(2)}) copy-start(s32[16,2]{0,1:T(2,128)} %param.7) | copy-start | bytes 388
  58.8 72.7 %copy-start = (f32[1,2,1024,128]{3,2,1,0:T(8,128)S(1)}, f32[1,2,1024,128]{3,2,1,0:T(8,128)}, u32[]{:S(2)}) copy-start(f32[1,2,1024,128]{3,2,1,0:T(8,128)} %param.6) | copy-start | bytes 3145732
  79.5 31.6 %collective-permute-start.3 = (bf16[8,2,32,640]{3,2,1,0:T(8,128)(2,1)S(1)}, bf16[8,2,32,640]{3,2,1,0:T(8,128)(2,1)S(1)}, u32[]{:S(2)}, u32[]{:S(2)}) collective-permute-start(bf16[8,2,32,640]{3,2,1,0:T(8,128)(2,1)S(1)} %all_to_all.11.refs_0_), channel_id=1, source_target_pairs={{24,0},{25,1},{26,2},{27,3},{28,4},{29,5},{30,6},{31,7},{0,8},{1,9... | collective-permute-start | bytes 1966088 | tf_op jit(solution)/shard_map/ppermute | solution.py:31
  81.9 33.3 %collective-permute-start.1 = (bf16[8,2,32,640]{3,2,1,0:T(8,128)(2,1)S(1)}, bf16[8,2,32,640]{3,2,1,0:T(8,128)(2,1)S(1)}, u32[]{:S(2)}, u32[]{:S(2)}) collective-permute-start(bf16[8,2,32,640]{3,2,1,0:T(8,128)(2,1)S(1)} %all_to_all.11.refs_0_), channel_id=1, source_target_pairs={{8,0},{9,1},{10,2},{11,3},{12,4},{13,5},{14,6},{15,7},{16,8},{17,9... | collective-permute-start | bytes 1966088 | tf_op jit(solution)/shard_map/ppermute | solution.py:31
  111.8 17.3 %collective-permute-start.4 = (bf16[4,2,32,640]{3,2,1,0:T(8,128)(2,1)}, bf16[4,2,32,640]{3,2,1,0:T(8,128)(2,1)S(1)}, u32[]{:S(2)}, u32[]{:S(2)}) collective-permute-start(bf16[4,2,32,640]{3,2,1,0:T(8,128)(2,1)} %slice.17), channel_id=1, source_target_pairs={{24,0},{25,1},{26,2},{27,3},{28,4},{29,5},{30,6},{31,7},{0,8},{1,9... | collective-permute-start | bytes 983048 | tf_op jit(solution)/shard_map/ppermute | solution.py:31
  116.0 15.4 %collective-permute-start.2 = (bf16[4,2,32,640]{3,2,1,0:T(8,128)(2,1)}, bf16[4,2,32,640]{3,2,1,0:T(8,128)(2,1)}, u32[]{:S(2)}, u32[]{:S(2)}) collective-permute-start(bf16[4,2,32,640]{3,2,1,0:T(8,128)(2,1)} %slice.16), channel_id=1, source_target_pairs={{8,0},{9,1},{10,2},{11,3},{12,4},{13,5},{14,6},{15,7},{16,8},{17,9... | collective-permute-start | bytes 983048 | tf_op jit(solution)/shard_map/ppermute | solution.py:31
Sparse Core Ops, SparseCore 0:
  11.8 46.7 all-gather.3
  60.7 70.7 all-gather.5

commit v5 on v4

--- a/solution.py
+++ b/solution.py
@@ -14,7 +14,6 @@
 PANEL = 32
 X_CHIPS, Z_CHIPS = 4, 8
 ALONG_Z = [[x * Z_CHIPS + z for z in range(Z_CHIPS)] for x in range(X_CHIPS)]
-ALONG_X = [[x * Z_CHIPS + z for x in range(X_CHIPS)] for z in range(Z_CHIPS)]
 
 
 def high_low(value):
@@ -42,7 +41,8 @@
     return own, after, across_low, across_high, before
 
 
-def fill_factor(x, pieces, factor):
+def fill_kernel(place, *refs):
+    x, pieces, factor = place[0], refs[:5], refs[5]
     own, after, across_low, across_high, before = pieces
     half = Z_CHIPS // 2
     blocks = factor.shape[1] // TILE
@@ -204,11 +204,9 @@
             end = start
 
 
-def eliminate_kernel(live, place, *refs):
-    pieces, basis, moment, out = refs[:5], refs[5], refs[6], refs[7]
-    factor, projected, transposed, system, work, done, inverse = refs[8:]
+def eliminate_kernel(live, factor, basis, moment, out, *scratch):
+    projected, transposed, system, work, done, inverse = scratch
     blocks = out.shape[1] // TILE
-    fill_factor(place[0], pieces, factor)
     normal_equations(basis, moment, factor, projected, transposed, system)
 
     def step(j, carry):
@@ -222,17 +220,31 @@
     lax.fori_loop(0, blocks, step, 0)
 
 
-def eliminate(live, place, pieces, basis, moment):
+def whole_factor(place, pieces):
+    order = X_CHIPS * Z_CHIPS * pieces[0].shape[2]
+    smem = pl.BlockSpec(memory_space=pltpu.SMEM)
+    vmem = pl.BlockSpec(memory_space=pltpu.VMEM)
+    return pl.pallas_call(
+        fill_kernel,
+        out_shape=jax.ShapeDtypeStruct((2, order, order), BF16),
+        in_specs=[smem] + [vmem] * 5,
+        out_specs=vmem,
+        compiler_params=pltpu.CompilerParams(vmem_limit_bytes=VMEM_BYTES),
+        cost_estimate=pl.CostEstimate(flops=0, bytes_accessed=7 << 20, transcendentals=0),
+        name="whole_factor",
+    )(place, *pieces)
+
+
+def eliminate(live, factor, basis, moment):
     _, order, width = moment.shape
     smem = pl.BlockSpec(memory_space=pltpu.SMEM)
     vmem = pl.BlockSpec(memory_space=pltpu.VMEM)
     return pl.pallas_call(
         eliminate_kernel,
         out_shape=jax.ShapeDtypeStruct((2, order, width), F32),
-        in_specs=[smem, smem] + [vmem] * 7,
+        in_specs=[smem] + [vmem] * 3,
         out_specs=vmem,
         scratch_shapes=[
-            pltpu.VMEM((2, order, order), BF16),
             pltpu.VMEM((2, order, order), BF16),
             pltpu.VMEM((2, order, order), BF16),
             pltpu.VMEM((2, order // TILE, TILE, order + width), F32),
@@ -243,7 +255,7 @@
         compiler_params=pltpu.CompilerParams(vmem_limit_bytes=VMEM_BYTES),
         cost_estimate=pl.CostEstimate(flops=10 * order**3, bytes_accessed=12 << 20, transcendentals=0),
         name="eliminate",
-    )(live, place, *pieces, basis, moment)
+    )(live, factor, basis, moment)
 
 
 def on_device(partial_stats, old_basis, exp_avg, slot_block):
@@ -251,7 +263,7 @@
     n_rows = slot_block.shape[0]
     group = lax.axis_index("group")
 
-    basis = lax.all_gather(old_basis[0], "group", axis=0, axis_index_groups=ALONG_Z)
+    basis = lax.all_gather(old_basis[0], "group", axis=0)
 
     kept = order // 2 + TILE
     block_start = group * slab_rows // TILE * TILE
@@ -269,14 +281,12 @@
     pairs = (shares_for(core).astype(F32) + other.astype(F32)).astype(BF16)
     same_core = [list(range(c, n_rows, 2)) for c in range(2)]
     shares = lax.all_to_all(pairs, "dp", split_axis=0, concat_axis=0, axis_index_groups=same_core)
-    shares, basis = lax.optimization_barrier((shares, basis))
-    basis = lax.all_gather(basis, "group", axis=0, axis_index_groups=ALONG_X)
-    basis = basis.reshape((X_CHIPS * Z_CHIPS,) + basis.shape[2:])
     factor = jnp.sum(shares.astype(F32), axis=0).astype(BF16)
 
     own_slots = lax.dynamic_index_in_dim(slot_block, lax.axis_index("dp"), 0, keepdims=False)
     place = jnp.stack([group // Z_CHIPS, group % Z_CHIPS]).astype(jnp.int32)
-    return eliminate(own_slots, place, gather_factor(factor), basis, exp_avg[0])[None]
+    factor = whole_factor(place, gather_factor(factor))
+    return eliminate(own_slots, factor, basis, exp_avg[0])[None]
 
 
 def solution(mesh):

time: 194 us -> 184 us (0.948)
  waiting for transfers between devices: 56.8 us -> 31.2 us
  blocking collectives: 48.2 us -> 57 us
  starting transfers between devices: 13.6 us -> 16 us
  Pallas kernels: 52.4 us -> 54.8 us
    all_gather x2 -> x1, waiting for transfers between devices: 17.3 us -> 0.01 us  [on_device(): basis = lax.all_gather(old_basis[0], 'group', axis=0)]
    ppermute x4, waiting for transfers between devices: 38.4 us -> 29.3 us  [from_neighbour(): return lax.ppermute(value, 'group', pairs)]
    all_to_all x1, blocking collectives: 20.7 us -> 29.5 us  [gather_factor(): lax.all_to_all(copies, 'group', split_axis=0, concat_axis=0, axis_index_g...]
    pallas_call x0 -> x1, Pallas kernels: none -> 3.48 us  [whole_factor(): pl.pallas_call(fill_kernel, out_shape=jax.ShapeDtypeStruct((2, order, ord...]
    unnamed x6 -> x8, local copies, waits for them, and re-layouts: 0.02 us -> 3.42 us
    ppermute x4, starting transfers between devices: 11.7 us -> 14.1 us  [from_neighbour(): return lax.ppermute(value, 'group', pairs)]
  transfers between devices with their start and end apart: 7 -> 6, of which waited for: 6 -> 4; matrix products, arithmetic and copies ran while one was open for 2% -> 3% of each run, Pallas kernels for 0% -> 2%
where the time goes in v5:
time: 184 us; the launch traced here: 181 us
  blocking collectives  57 us (31%)
  Pallas kernels  54.8 us (30%)
  waiting for transfers between devices  31.2 us (17%)
  starting transfers between devices  16 us (9%)
  between operations  13.6 us (7%)
  local copies, waits for them, and re-layouts  6.72 us (4%)
    pallas_call x1, Pallas kernels, eliminate(): pl.pallas_call(eliminate_kernel, out_shape=jax.ShapeDtypeStruct((2, order...  51.3 us
    all_to_all x1, blocking collectives, gather_factor(): lax.all_to_all(copies, 'group', split_axis=0, concat_axis=0, axis_index_g...  29.5 us
    ppermute x4, waiting for transfers between devices, from_neighbour(): return lax.ppermute(value, 'group', pairs)  29.3 us
    all_to_all x1, blocking collectives, on_device(): lax.all_to_all(pairs, 'dp', split_axis=0, concat_axis=0, axis_index_group...  27.5 us
    ppermute x4, starting transfers between devices, from_neighbour(): return lax.ppermute(value, 'group', pairs)  14.1 us
  transfers between devices with their start and end apart: 6, of which 4 were waited for; matrix products, arithmetic and copies ran while one was open for 3% of the time, Pallas kernels for 2%

profile of v5, /device:TPU:6, one launch (start us, length us, event | category | flops | bytes accessed | tf_op | source)
XLA Modules:
  0.0 180.6 jit_solution(5178655727442739514)
XLA Ops:
  6.5 0.7 all-gather.2.cloned.1.call-update
  7.3 0.7 broadcast_maximum_fusion
  8.0 0.1 reshape.16
  8.0 0.1 constant_dynamic-slice_fusion
  8.1 0.1 copy.10
  8.3 0.1 reshape.29
  8.4 1.1 slice_bitcast_fusion
  9.4 0.3 fusion.1
  9.7 0.7 gather_fusion.1
  10.4 1.9 %collective-permute-start = (bf16[8,2,32,640]{3,2,1,0:T(8,128)(2,1)S(1)}, bf16[8,2,32,640]{3,2,1,0:T(8,128)(2,1)S(1)}, u32[]{:S(2)}, u32[]{:S(2)}) collective-permute-start(bf16[8,2,32,640]{3,2,1,0:T(8,128)(2,1)S(1)} %bitcast.19), channel_id=1, source_target_pairs={{0,32},{32,0},{64,96},{96,64},{128,160},{160,128},{192,224},{224,1... | collective-permute-start | bytes 1966088 | tf_op jit(solution)/shard_map/ppermute | solution.py:280
  12.3 0.1 copy.9
  12.5 0.1 reshape.21
  12.6 0.7 gather_fusion
  13.2 1.2 collective-permute-done
  14.4 0.2 fusion
  14.6 27.5 %all_to_all.10 = bf16[8,2,32,640]{3,2,1,0:T(8,128)(2,1)S(1)} all-to-all(bf16[8,2,32,640]{3,2,1,0:T(8,128)(2,1)S(1)} %fusion), channel_id=1, replica_groups={{0,64,128,192,256,320,384,448},{32,96,160,224,288,352,416,480},{1,65,12..., dimensions={0} | all-to-all | bytes 1310720 | tf_op jit(solution)/shard_map/all_to_all | solution.py:283
  42.1 0.1 reduce_sum.12
  42.2 0.1 broadcast_in_dim.18
  42.3 29.5 %all_to_all.11.refs_0_ = bf16[8,2,32,640]{3,2,1,0:T(8,128)(2,1)S(1)} all-to-all(bf16[8,2,32,640]{3,2,1,0:T(8,128)(2,1)S(1)} %broadcast_in_dim.18), channel_id=1, replica_groups={{0,1,2,3,4,5,6,7},{8,9,10,11,12,13,14,15},{16,17,18,19,20,21,22,23},{24..., dimensions={0} | all-to-all | bytes 1310720 | tf_op jit(solution)/shard_map/all_to_all | solution.py:35
  71.8 2.7 %collective-permute-start.1 = (bf16[8,2,32,640]{3,2,1,0:T(8,128)(2,1)S(1)}, bf16[8,2,32,640]{3,2,1,0:T(8,128)(2,1)S(1)}, u32[]{:S(2)}, u32[]{:S(2)}) collective-permute-start(bf16[8,2,32,640]{3,2,1,0:T(8,128)(2,1)S(1)} %all_to_all.11.refs_0_), channel_id=1, source_target_pairs={{8,0},{9,1},{10,2},{11,3},{12,4},{13,5},{14,6},{15,7},{16,8},{17,9... | collective-permute-start | bytes 1966088 | tf_op jit(solution)/shard_map/ppermute | solution.py:30
  74.5 4.3 %collective-permute-start.3 = (bf16[8,2,32,640]{3,2,1,0:T(8,128)(2,1)S(1)}, bf16[8,2,32,640]{3,2,1,0:T(8,128)(2,1)S(1)}, u32[]{:S(2)}, u32[]{:S(2)}) collective-permute-start(bf16[8,2,32,640]{3,2,1,0:T(8,128)(2,1)S(1)} %all_to_all.11.refs_0_), channel_id=1, source_target_pairs={{24,0},{25,1},{26,2},{27,3},{28,4},{29,5},{30,6},{31,7},{0,8},{1,9... | collective-permute-start | bytes 1966088 | tf_op jit(solution)/shard_map/ppermute | solution.py:30
  78.8 24.8 %collective-permute-done.1.refs_1_ = bf16[8,2,32,640]{3,2,1,0:T(8,128)(2,1)S(1)} collective-permute-done((bf16[8,2,32,640]{3,2,1,0:T(8,128)(2,1)S(1)}, bf16[8,2,32,640]{3,2,1,0:T(8,128)(2,1)S(1)}, u32[]{:S(2)}, u32[]{:S(2)}) %collective-permute-start.1) | collective-permute-done | bytes 655392 | tf_op jit(solution)/shard_map/ppermute | solution.py:30
  103.6 2.9 %collective-permute-start.2 = (bf16[4,2,32,640]{3,2,1,0:T(8,128)(2,1)S(1)}, bf16[4,2,32,640]{3,2,1,0:T(8,128)(2,1)S(1)}, u32[]{:S(2)}, u32[]{:S(2)}) collective-permute-start(bf16[4,2,32,640]{3,2,1,0:T(8,128)(2,1)S(1)} %slice.16), channel_id=1, source_target_pairs={{8,0},{9,1},{10,2},{11,3},{12,4},{13,5},{14,6},{15,7},{16,8},{17,9... | collective-permute-start | bytes 983048 | tf_op jit(solution)/shard_map/ppermute | solution.py:30
  106.6 4.2 %collective-permute-start.4 = (bf16[4,2,32,640]{3,2,1,0:T(8,128)(2,1)S(1)}, bf16[4,2,32,640]{3,2,1,0:T(8,128)(2,1)S(1)}, u32[]{:S(2)}, u32[]{:S(2)}) collective-permute-start(bf16[4,2,32,640]{3,2,1,0:T(8,128)(2,1)S(1)} %slice.17), channel_id=1, source_target_pairs={{24,0},{25,1},{26,2},{27,3},{28,4},{29,5},{30,6},{31,7},{0,8},{1,9... | collective-permute-start | bytes 983048 | tf_op jit(solution)/shard_map/ppermute | solution.py:30
  110.8 0.2 fusion.2.live
  111.0 0.1 pad_add_fusion.place
  111.1 2.8 %collective-permute-done.2.refs_2_ = bf16[4,2,32,640]{3,2,1,0:T(8,128)(2,1)S(1)} collective-permute-done((bf16[4,2,32,640]{3,2,1,0:T(8,128)(2,1)S(1)}, bf16[4,2,32,640]{3,2,1,0:T(8,128)(2,1)S(1)}, u32[]{:S(2)}, u32[]{:S(2)}) %collective-permute-start.2) | collective-permute-done | bytes 327712 | tf_op jit(solution)/shard_map/ppermute | solution.py:30
  113.8 1.7 collective-permute-done.4.refs_3_
  115.6 3.5 %whole_factor.1.factor = bf16[2,1024,1024]{2,1,0:T(8,128)(2,1)} custom-call(s32[2]{0:T(128)S(1)} %pad_add_fusion.place, bf16[8,2,32,640]{3,2,1,0:T(8,128)(2,1)S(1)} %all_to_all.11.refs_0_, bf16[8,2,32,640]{3,2,1,0:T(8,128)(2,1)S(1)} %collective-permute-done.1.refs_1_, bf16[4,2,32,640]{3,2,1,0:T(8,128)(2,1)S(1)} %collective-permute-done.2.refs_2_, ...), custom_call_target="tpu_custom_call" | custom-call | bytes 7340032 | tf_op jit(solution)/shard_map/whole_factor/pallas_call | solution.py:227
  119.0 2.2 %copy-done = bf16[2,1024,1024]{2,1,0:T(8,128)(2,1)S(1)} copy-done((bf16[2,1024,1024]{2,1,0:T(8,128)(2,1)S(1)}, bf16[2,1024,1024]{2,1,0:T(8,128)(2,1)}, u32[]{:S(2)}) %copy-start) | copy-done | bytes 4194328
  121.2 1.2 copy-done.1
  122.5 51.3 %eliminate.1 = f32[2,1024,128]{2,1,0:T(8,128)} custom-call(s32[2]{0:T(128)S(1)} %fusion.2.live, bf16[2,1024,1024]{2,1,0:T(8,128)(2,1)S(1)} %copy-done, bf16[32,2,32,1024]{3,2,1,0:T(8,128)(2,1)} %all-gather.2.cloned.1.call-done.basis, f32[2,1024,128]{2,1,0:T(8,128)S(1)} %bitcast.16), custom_call_target="tpu_custom_call" | custom-call | flops 10737418240 | bytes 12582912 | tf_op jit(solution)/shard_map/eliminate/pallas_call | solution.py:242
  (13 shorter events, 0.1 us)
Async XLA Ops:
  6.5 2.9 %copy-start.2 = (bf16[1,16,32,1024]{3,2,1,0:T(8,128)(2,1)S(1)}, bf16[1,16,32,1024]{3,2,1,0:T(8,128)(2,1)}, u32[]{:S(2)}) copy-start(bf16[1,16,32,1024]{3,2,1,0:T(8,128)(2,1)} %param.4) | copy-start | bytes 3145732
  6.5 112.5 %all-gather.2.cloned.1.call-start = ((), (), s32[]{:S(2)}) async-start(), calls=%async_computation.2 | async-start | bytes 4325376 | tf_op jit(solution)/shard_map/all_gather | solution.py:266
  10.4 4.0 %collective-permute-start = (bf16[8,2,32,640]{3,2,1,0:T(8,128)(2,1)S(1)}, bf16[8,2,32,640]{3,2,1,0:T(8,128)(2,1)S(1)}, u32[]{:S(2)}, u32[]{:S(2)}) collective-permute-start(bf16[8,2,32,640]{3,2,1,0:T(8,128)(2,1)S(1)} %bitcast.19), channel_id=1, source_target_pairs={{0,32},{32,0},{64,96},{96,64},{128,160},{160,128},{192,224},{224,1... | collective-permute-start | bytes 1966088 | tf_op jit(solution)/shard_map/ppermute | solution.py:280
  42.2 68.5 %copy-start.3 = (s32[16,2]{0,1:T(2,128)S(1)}, s32[16,2]{0,1:T(2,128)}, u32[]{:S(2)}) copy-start(s32[16,2]{0,1:T(2,128)} %param.7) | copy-start | bytes 388
  71.8 31.8 %collective-permute-start.1 = (bf16[8,2,32,640]{3,2,1,0:T(8,128)(2,1)S(1)}, bf16[8,2,32,640]{3,2,1,0:T(8,128)(2,1)S(1)}, u32[]{:S(2)}, u32[]{:S(2)}) collective-permute-start(bf16[8,2,32,640]{3,2,1,0:T(8,128)(2,1)S(1)} %all_to_all.11.refs_0_), channel_id=1, source_target_pairs={{8,0},{9,1},{10,2},{11,3},{12,4},{13,5},{14,6},{15,7},{16,8},{17,9... | collective-permute-start | bytes 1966088 | tf_op jit(solution)/shard_map/ppermute | solution.py:30
  74.5 32.1 %collective-permute-start.3 = (bf16[8,2,32,640]{3,2,1,0:T(8,128)(2,1)S(1)}, bf16[8,2,32,640]{3,2,1,0:T(8,128)(2,1)S(1)}, u32[]{:S(2)}, u32[]{:S(2)}) collective-permute-start(bf16[8,2,32,640]{3,2,1,0:T(8,128)(2,1)S(1)} %all_to_all.11.refs_0_), channel_id=1, source_target_pairs={{24,0},{25,1},{26,2},{27,3},{28,4},{29,5},{30,6},{31,7},{0,8},{1,9... | collective-permute-start | bytes 1966088 | tf_op jit(solution)/shard_map/ppermute | solution.py:30
  103.6 10.2 %collective-permute-start.2 = (bf16[4,2,32,640]{3,2,1,0:T(8,128)(2,1)S(1)}, bf16[4,2,32,640]{3,2,1,0:T(8,128)(2,1)S(1)}, u32[]{:S(2)}, u32[]{:S(2)}) collective-permute-start(bf16[4,2,32,640]{3,2,1,0:T(8,128)(2,1)S(1)} %slice.16), channel_id=1, source_target_pairs={{8,0},{9,1},{10,2},{11,3},{12,4},{13,5},{14,6},{15,7},{16,8},{17,9... | collective-permute-start | bytes 983048 | tf_op jit(solution)/shard_map/ppermute | solution.py:30
  106.6 9.0 %collective-permute-start.4 = (bf16[4,2,32,640]{3,2,1,0:T(8,128)(2,1)S(1)}, bf16[4,2,32,640]{3,2,1,0:T(8,128)(2,1)S(1)}, u32[]{:S(2)}, u32[]{:S(2)}) collective-permute-start(bf16[4,2,32,640]{3,2,1,0:T(8,128)(2,1)S(1)} %slice.17), channel_id=1, source_target_pairs={{24,0},{25,1},{26,2},{27,3},{28,4},{29,5},{30,6},{31,7},{0,8},{1,9... | collective-permute-start | bytes 983048 | tf_op jit(solution)/shard_map/ppermute | solution.py:30
  119.0 2.2 %copy-start = (bf16[2,1024,1024]{2,1,0:T(8,128)(2,1)S(1)}, bf16[2,1024,1024]{2,1,0:T(8,128)(2,1)}, u32[]{:S(2)}) copy-start(bf16[2,1024,1024]{2,1,0:T(8,128)(2,1)} %whole_factor.1.factor) | copy-start | bytes 12582916
  121.2 1.2 copy-start.1
Sparse Core Ops, SparseCore 0:
  10.5 102.9 all-gather.1

commit v6 on v4

--- a/solution.py
+++ b/solution.py
@@ -14,7 +14,6 @@
 PANEL = 32
 X_CHIPS, Z_CHIPS = 4, 8
 ALONG_Z = [[x * Z_CHIPS + z for z in range(Z_CHIPS)] for x in range(X_CHIPS)]
-ALONG_X = [[x * Z_CHIPS + z for x in range(X_CHIPS)] for z in range(Z_CHIPS)]
 
 
 def high_low(value):
@@ -34,16 +33,17 @@
 def gather_factor(slab):
     copies = jnp.broadcast_to(slab[None], (Z_CHIPS,) + slab.shape)
     own = lax.all_to_all(copies, "group", split_axis=0, concat_axis=0, axis_index_groups=ALONG_Z)
-    after = from_neighbour(own, 1, 0)
-    before = from_neighbour(own, -1, 0)
-    half = Z_CHIPS // 2
-    across_low = from_neighbour(after[:half], 1, 0)
-    across_high = from_neighbour(before[half:], -1, 0)
-    return own, after, across_low, across_high, before
+    low, high = own[: Z_CHIPS // 2], own[Z_CHIPS // 2 :]
+    after_low = from_neighbour(low, 1, 0)
+    before_high = from_neighbour(high, -1, 0)
+    after_high = from_neighbour(high, 1, 0)
+    before_low = from_neighbour(low, -1, 0)
+    across_low = from_neighbour(after_low, 1, 0)
+    across_high = from_neighbour(before_high, -1, 0)
+    return own, after_low, after_high, across_low, across_high, before_low, before_high
 
 
 def fill_factor(x, pieces, factor):
-    own, after, across_low, across_high, before = pieces
     half = Z_CHIPS // 2
     blocks = factor.shape[1] // TILE
     for distance in range(X_CHIPS):
@@ -51,10 +51,10 @@
             block_row = lax.rem(x + distance, X_CHIPS) * 2 + z_half
             here = pl.ds(pl.multiple_of(block_row * TILE, TILE), TILE)
             for slot in range(2):
-                if distance == 2:
-                    piece = (across_low, across_high)[z_half][:, slot]
+                if distance == 0:
+                    piece = pieces[0][half * z_half : half * (z_half + 1), slot]
                 else:
-                    piece = (own, after, None, before)[distance][half * z_half : half * (z_half + 1), slot]
+                    piece = pieces[2 * distance - 1 + z_half][:, slot]
                 piece = piece.reshape(TILE, piece.shape[2])
                 for k in range(blocks // 2 + 1):
                     there = pl.ds(pl.multiple_of(lax.rem(block_row + k, blocks) * TILE, TILE), TILE)
@@ -205,8 +205,8 @@
 
 
 def eliminate_kernel(live, place, *refs):
-    pieces, basis, moment, out = refs[:5], refs[5], refs[6], refs[7]
-    factor, projected, transposed, system, work, done, inverse = refs[8:]
+    pieces, basis, moment, out = refs[:7], refs[7], refs[8], refs[9]
+    factor, projected, transposed, system, work, done, inverse = refs[10:]
     blocks = out.shape[1] // TILE
     fill_factor(place[0], pieces, factor)
     normal_equations(basis, moment, factor, projected, transposed, system)
@@ -229,7 +229,7 @@
     return pl.pallas_call(
         eliminate_kernel,
         out_shape=jax.ShapeDtypeStruct((2, order, width), F32),
-        in_specs=[smem, smem] + [vmem] * 7,
+        in_specs=[smem, smem] + [vmem] * 9,
         out_specs=vmem,
         scratch_shapes=[
             pltpu.VMEM((2, order, order), BF16),
@@ -251,7 +251,7 @@
     n_rows = slot_block.shape[0]
     group = lax.axis_index("group")
 
-    basis = lax.all_gather(old_basis[0], "group", axis=0, axis_index_groups=ALONG_Z)
+    basis = lax.all_gather(old_basis[0], "group", axis=0)
 
     kept = order // 2 + TILE
     block_start = group * slab_rows // TILE * TILE
@@ -269,9 +269,6 @@
     pairs = (shares_for(core).astype(F32) + other.astype(F32)).astype(BF16)
     same_core = [list(range(c, n_rows, 2)) for c in range(2)]
     shares = lax.all_to_all(pairs, "dp", split_axis=0, concat_axis=0, axis_index_groups=same_core)
-    shares, basis = lax.optimization_barrier((shares, basis))
-    basis = lax.all_gather(basis, "group", axis=0, axis_index_groups=ALONG_X)
-    basis = basis.reshape((X_CHIPS * Z_CHIPS,) + basis.shape[2:])
     factor = jnp.sum(shares.astype(F32), axis=0).astype(BF16)
 
     own_slots = lax.dynamic_index_in_dim(slot_block, lax.axis_index("dp"), 0, keepdims=False)

time: 194 us -> 177 us (0.912)
  waiting for transfers between devices: 56.8 us -> 24.9 us
  blocking collectives: 48.2 us -> 57.1 us
  starting transfers between devices: 13.6 us -> 20.6 us
    ppermute x4 -> x6, waiting for transfers between devices: 38.4 us -> 19.6 us  [from_neighbour(): return lax.ppermute(value, 'group', pairs)]
    all_gather x2 -> x1, waiting for transfers between devices: 17.3 us -> 3.44 us  [on_device(): basis = lax.all_gather(old_basis[0], 'group', axis=0)]
    all_to_all x1, blocking collectives: 20.7 us -> 29.6 us  [gather_factor(): lax.all_to_all(copies, 'group', split_axis=0, concat_axis=0, axis_index_g...]
    ppermute x4 -> x6, starting transfers between devices: 11.7 us -> 18.7 us  [from_neighbour(): return lax.ppermute(value, 'group', pairs)]
  transfers between devices with their start and end apart: 7 -> 8, of which waited for: 6 -> 6; matrix products, arithmetic and copies ran while one was open for 2% -> 3% of each run, Pallas kernels for 0% -> 0%
where the time goes in v6:
time: 177 us; the launch traced here: 174 us
  blocking collectives  57.1 us (32%)
  Pallas kernels  52.4 us (30%)
  waiting for transfers between devices  24.9 us (14%)
  starting transfers between devices  20.6 us (12%)
  between operations  13.6 us (8%)
  local copies, waits for them, and re-layouts  4.15 us (2%)
    pallas_call x1, Pallas kernels, eliminate(): pl.pallas_call(eliminate_kernel, out_shape=jax.ShapeDtypeStruct((2, order...  52.4 us
    all_to_all x1, blocking collectives, gather_factor(): lax.all_to_all(copies, 'group', split_axis=0, concat_axis=0, axis_index_g...  29.6 us
    all_to_all x1, blocking collectives, on_device(): lax.all_to_all(pairs, 'dp', split_axis=0, concat_axis=0, axis_index_group...  27.5 us
    ppermute x6, waiting for transfers between devices, from_neighbour(): return lax.ppermute(value, 'group', pairs)  19.6 us
    ppermute x6, starting transfers between devices, from_neighbour(): return lax.ppermute(value, 'group', pairs)  18.7 us
  transfers between devices with their start and end apart: 8, of which 6 were waited for; matrix products, arithmetic and copies ran while one was open for 3% of the time, Pallas kernels for 0%

profile of v6, /device:TPU:6, one launch (start us, length us, event | category | flops | bytes accessed | tf_op | source)
XLA Modules:
  0.0 174.2 jit_solution(17867074607270527433)
XLA Ops:
  6.5 0.7 all-gather.2.cloned.1.call-update
  7.3 0.7 broadcast_maximum_fusion
  8.0 0.1 reshape.16
  8.1 0.1 copy.10
  8.3 0.1 reshape.29
  8.4 1.1 slice_bitcast_fusion
  9.4 0.3 fusion.1
  9.7 0.7 gather_fusion.1
  10.4 1.9 %collective-permute-start = (bf16[8,2,32,640]{3,2,1,0:T(8,128)(2,1)S(1)}, bf16[8,2,32,640]{3,2,1,0:T(8,128)(2,1)S(1)}, u32[]{:S(2)}, u32[]{:S(2)}) collective-permute-start(bf16[8,2,32,640]{3,2,1,0:T(8,128)(2,1)S(1)} %bitcast.19), channel_id=1, source_target_pairs={{0,32},{32,0},{64,96},{96,64},{128,160},{160,128},{192,224},{224,1... | collective-permute-start | bytes 1966088 | tf_op jit(solution)/shard_map/ppermute | solution.py:268
  12.3 0.1 copy.9
  12.5 0.1 reshape.21
  12.6 0.7 gather_fusion
  13.2 1.2 collective-permute-done
  14.4 0.2 fusion
  14.6 27.5 %all_to_all.10 = bf16[8,2,32,640]{3,2,1,0:T(8,128)(2,1)S(1)} all-to-all(bf16[8,2,32,640]{3,2,1,0:T(8,128)(2,1)S(1)} %fusion), channel_id=1, replica_groups={{0,64,128,192,256,320,384,448},{32,96,160,224,288,352,416,480},{1,65,12..., dimensions={0} | all-to-all | bytes 1310720 | tf_op jit(solution)/shard_map/all_to_all | solution.py:271
  42.1 0.1 reduce_sum.12
  42.3 29.6 %all_to_all.11.refs_0_ = bf16[8,2,32,640]{3,2,1,0:T(8,128)(2,1)S(1)} all-to-all(bf16[8,2,32,640]{3,2,1,0:T(8,128)(2,1)S(1)} %broadcast_in_dim.18), channel_id=1, replica_groups={{0,1,2,3,4,5,6,7},{8,9,10,11,12,13,14,15},{16,17,18,19,20,21,22,23},{24..., dimensions={0} | all-to-all | bytes 1310720 | tf_op jit(solution)/shard_map/all_to_all | solution.py:35
  71.9 0.9 fusion.3
  72.8 2.5 %collective-permute-start.4 = (bf16[4,2,32,640]{3,2,1,0:T(8,128)(2,1)}, bf16[4,2,32,640]{3,2,1,0:T(8,128)(2,1)S(1)}, u32[]{:S(2)}, u32[]{:S(2)}) collective-permute-start(bf16[4,2,32,640]{3,2,1,0:T(8,128)(2,1)} %get-tuple-element.5), channel_id=1, source_target_pairs={{24,0},{25,1},{26,2},{27,3},{28,4},{29,5},{30,6},{31,7},{0,8},{1,9... | collective-permute-start | bytes 983048 | tf_op jit(solution)/shard_map/ppermute | solution.py:30
  75.3 3.3 %collective-permute-start.1 = (bf16[4,2,32,640]{3,2,1,0:T(8,128)(2,1)}, bf16[4,2,32,640]{3,2,1,0:T(8,128)(2,1)S(1)}, u32[]{:S(2)}, u32[]{:S(2)}) collective-permute-start(bf16[4,2,32,640]{3,2,1,0:T(8,128)(2,1)} %get-tuple-element.6), channel_id=1, source_target_pairs={{8,0},{9,1},{10,2},{11,3},{12,4},{13,5},{14,6},{15,7},{16,8},{17,9... | collective-permute-start | bytes 983048 | tf_op jit(solution)/shard_map/ppermute | solution.py:30
  78.6 2.7 %collective-permute-start.2 = (bf16[4,2,32,640]{3,2,1,0:T(8,128)(2,1)}, bf16[4,2,32,640]{3,2,1,0:T(8,128)(2,1)S(1)}, u32[]{:S(2)}, u32[]{:S(2)}) collective-permute-start(bf16[4,2,32,640]{3,2,1,0:T(8,128)(2,1)} %get-tuple-element.5), channel_id=1, source_target_pairs={{8,0},{9,1},{10,2},{11,3},{12,4},{13,5},{14,6},{15,7},{16,8},{17,9... | collective-permute-start | bytes 983048 | tf_op jit(solution)/shard_map/ppermute | solution.py:30
  81.4 4.3 %collective-permute-start.6 = (bf16[4,2,32,640]{3,2,1,0:T(8,128)(2,1)}, bf16[4,2,32,640]{3,2,1,0:T(8,128)(2,1)S(1)}, u32[]{:S(2)}, u32[]{:S(2)}) collective-permute-start(bf16[4,2,32,640]{3,2,1,0:T(8,128)(2,1)} %get-tuple-element.6), channel_id=1, source_target_pairs={{24,0},{25,1},{26,2},{27,3},{28,4},{29,5},{30,6},{31,7},{0,8},{1,9... | collective-permute-start | bytes 983048 | tf_op jit(solution)/shard_map/ppermute | solution.py:30
  85.7 6.7 %collective-permute-done.4.refs_6_ = bf16[4,2,32,640]{3,2,1,0:T(8,128)(2,1)S(1)} collective-permute-done((bf16[4,2,32,640]{3,2,1,0:T(8,128)(2,1)}, bf16[4,2,32,640]{3,2,1,0:T(8,128)(2,1)S(1)}, u32[]{:S(2)}, u32[]{:S(2)}) %collective-permute-start.4) | collective-permute-done | bytes 327712 | tf_op jit(solution)/shard_map/ppermute | solution.py:30
  92.4 3.7 %collective-permute-start.5 = (bf16[4,2,32,640]{3,2,1,0:T(8,128)(2,1)S(1)}, bf16[4,2,32,640]{3,2,1,0:T(8,128)(2,1)S(1)}, u32[]{:S(2)}, u32[]{:S(2)}) collective-permute-start(bf16[4,2,32,640]{3,2,1,0:T(8,128)(2,1)S(1)} %collective-permute-done.4.refs_6_), channel_id=1, source_target_pairs={{24,0},{25,1},{26,2},{27,3},{28,4},{29,5},{30,6},{31,7},{0,8},{1,9... | collective-permute-start | bytes 983048 | tf_op jit(solution)/shard_map/ppermute | solution.py:30
  96.2 2.1 %collective-permute-start.3 = (bf16[4,2,32,640]{3,2,1,0:T(8,128)(2,1)S(1)}, bf16[4,2,32,640]{3,2,1,0:T(8,128)(2,1)}, u32[]{:S(2)}, u32[]{:S(2)}) collective-permute-start(bf16[4,2,32,640]{3,2,1,0:T(8,128)(2,1)S(1)} %collective-permute-done.1.refs_1_), channel_id=1, source_target_pairs={{8,0},{9,1},{10,2},{11,3},{12,4},{13,5},{14,6},{15,7},{16,8},{17,9... | collective-permute-start | bytes 983048 | tf_op jit(solution)/shard_map/ppermute | solution.py:30
  98.3 0.2 fusion.2.live
  98.5 0.1 pad_add_fusion.place
  98.6 6.8 %collective-permute-done.2.refs_2_ = bf16[4,2,32,640]{3,2,1,0:T(8,128)(2,1)S(1)} collective-permute-done((bf16[4,2,32,640]{3,2,1,0:T(8,128)(2,1)}, bf16[4,2,32,640]{3,2,1,0:T(8,128)(2,1)S(1)}, u32[]{:S(2)}, u32[]{:S(2)}) %collective-permute-start.2) | collective-permute-done | bytes 327712 | tf_op jit(solution)/shard_map/ppermute | solution.py:30
  105.4 0.4 collective-permute-done.6.refs_5_
  105.8 5.7 %collective-permute-done.5.refs_4_ = bf16[4,2,32,640]{3,2,1,0:T(8,128)(2,1)S(1)} collective-permute-done((bf16[4,2,32,640]{3,2,1,0:T(8,128)(2,1)S(1)}, bf16[4,2,32,640]{3,2,1,0:T(8,128)(2,1)S(1)}, u32[]{:S(2)}, u32[]{:S(2)}) %collective-permute-start.5) | collective-permute-done | bytes 327712 | tf_op jit(solution)/shard_map/ppermute | solution.py:30
  111.5 3.4 %all-gather.2.cloned.1.call-done.refs_7_ = bf16[32,2,32,1024]{3,2,1,0:T(8,128)(2,1)} async-done(((bf16[1,2,32,1024]{3,2,1,0:T(8,128)(2,1)}), bf16[32,2,32,1024]{3,2,1,0:T(8,128)(2,1)}) %all-gather.2.cloned.1.call-update) | async-done | bytes 4194320 | tf_op jit(solution)/shard_map/all_gather | solution.py:254
  114.9 52.4 %eliminate.1 = f32[2,1024,128]{2,1,0:T(8,128)} custom-call(s32[2]{0:T(128)S(1)} %fusion.2.live, s32[2]{0:T(128)S(1)} %pad_add_fusion.place, bf16[8,2,32,640]{3,2,1,0:T(8,128)(2,1)S(1)} %all_to_all.11.refs_0_, bf16[4,2,32,640]{3,2,1,0:T(8,128)(2,1)S(1)} %collective-permute-done.1.refs_1_, bf16[4,2,32,640]{3,2,1,0:T(8,128)(2,1)S(1)} %collective-permute-done.2.refs_2_, ...), custom_call_target="tpu_custom_call" | custom-call | flops 10737418240 | bytes 12582912 | tf_op jit(solution)/shard_map/eliminate/pallas_call | solution.py:229
  (13 shorter events, 0.2 us)
Async XLA Ops:
  6.5 2.9 %copy-start.1 = (bf16[1,16,32,1024]{3,2,1,0:T(8,128)(2,1)S(1)}, bf16[1,16,32,1024]{3,2,1,0:T(8,128)(2,1)}, u32[]{:S(2)}) copy-start(bf16[1,16,32,1024]{3,2,1,0:T(8,128)(2,1)} %param.4) | copy-start | bytes 3145732
  6.5 108.4 %all-gather.2.cloned.1.call-start = ((), (), s32[]{:S(2)}) async-start(), calls=%async_computation.2 | async-start | bytes 4325376 | tf_op jit(solution)/shard_map/all_gather | solution.py:254
  10.4 4.0 %collective-permute-start = (bf16[8,2,32,640]{3,2,1,0:T(8,128)(2,1)S(1)}, bf16[8,2,32,640]{3,2,1,0:T(8,128)(2,1)S(1)}, u32[]{:S(2)}, u32[]{:S(2)}) collective-permute-start(bf16[8,2,32,640]{3,2,1,0:T(8,128)(2,1)S(1)} %bitcast.19), channel_id=1, source_target_pairs={{0,32},{32,0},{64,96},{96,64},{128,160},{160,128},{192,224},{224,1... | collective-permute-start | bytes 1966088 | tf_op jit(solution)/shard_map/ppermute | solution.py:268
  42.2 56.1 %copy-start.2 = (s32[16,2]{0,1:T(2,128)S(1)}, s32[16,2]{0,1:T(2,128)}, u32[]{:S(2)}) copy-start(s32[16,2]{0,1:T(2,128)} %param.7) | copy-start | bytes 388
  42.3 72.7 %copy-start = (f32[1,2,1024,128]{3,2,1,0:T(8,128)S(1)}, f32[1,2,1024,128]{3,2,1,0:T(8,128)}, u32[]{:S(2)}) copy-start(f32[1,2,1024,128]{3,2,1,0:T(8,128)} %param.6) | copy-start | bytes 3145732
  72.8 19.7 %collective-permute-start.4 = (bf16[4,2,32,640]{3,2,1,0:T(8,128)(2,1)}, bf16[4,2,32,640]{3,2,1,0:T(8,128)(2,1)S(1)}, u32[]{:S(2)}, u32[]{:S(2)}) collective-permute-start(bf16[4,2,32,640]{3,2,1,0:T(8,128)(2,1)} %get-tuple-element.5), channel_id=1, source_target_pairs={{24,0},{25,1},{26,2},{27,3},{28,4},{29,5},{30,6},{31,7},{0,8},{1,9... | collective-permute-start | bytes 983048 | tf_op jit(solution)/shard_map/ppermute | solution.py:30
  75.3 20.9 %collective-permute-start.1 = (bf16[4,2,32,640]{3,2,1,0:T(8,128)(2,1)}, bf16[4,2,32,640]{3,2,1,0:T(8,128)(2,1)S(1)}, u32[]{:S(2)}, u32[]{:S(2)}) collective-permute-start(bf16[4,2,32,640]{3,2,1,0:T(8,128)(2,1)} %get-tuple-element.6), channel_id=1, source_target_pairs={{8,0},{9,1},{10,2},{11,3},{12,4},{13,5},{14,6},{15,7},{16,8},{17,9... | collective-permute-start | bytes 983048 | tf_op jit(solution)/shard_map/ppermute | solution.py:30
  78.6 26.7 %collective-permute-start.2 = (bf16[4,2,32,640]{3,2,1,0:T(8,128)(2,1)}, bf16[4,2,32,640]{3,2,1,0:T(8,128)(2,1)S(1)}, u32[]{:S(2)}, u32[]{:S(2)}) collective-permute-start(bf16[4,2,32,640]{3,2,1,0:T(8,128)(2,1)} %get-tuple-element.5), channel_id=1, source_target_pairs={{8,0},{9,1},{10,2},{11,3},{12,4},{13,5},{14,6},{15,7},{16,8},{17,9... | collective-permute-start | bytes 983048 | tf_op jit(solution)/shard_map/ppermute | solution.py:30
  81.4 24.4 %collective-permute-start.6 = (bf16[4,2,32,640]{3,2,1,0:T(8,128)(2,1)}, bf16[4,2,32,640]{3,2,1,0:T(8,128)(2,1)S(1)}, u32[]{:S(2)}, u32[]{:S(2)}) collective-permute-start(bf16[4,2,32,640]{3,2,1,0:T(8,128)(2,1)} %get-tuple-element.6), channel_id=1, source_target_pairs={{24,0},{25,1},{26,2},{27,3},{28,4},{29,5},{30,6},{31,7},{0,8},{1,9... | collective-permute-start | bytes 983048 | tf_op jit(solution)/shard_map/ppermute | solution.py:30
  92.4 19.0 %collective-permute-start.5 = (bf16[4,2,32,640]{3,2,1,0:T(8,128)(2,1)S(1)}, bf16[4,2,32,640]{3,2,1,0:T(8,128)(2,1)S(1)}, u32[]{:S(2)}, u32[]{:S(2)}) collective-permute-start(bf16[4,2,32,640]{3,2,1,0:T(8,128)(2,1)S(1)} %collective-permute-done.4.refs_6_), channel_id=1, source_target_pairs={{24,0},{25,1},{26,2},{27,3},{28,4},{29,5},{30,6},{31,7},{0,8},{1,9... | collective-permute-start | bytes 983048 | tf_op jit(solution)/shard_map/ppermute | solution.py:30
  96.2 15.3 %collective-permute-start.3 = (bf16[4,2,32,640]{3,2,1,0:T(8,128)(2,1)S(1)}, bf16[4,2,32,640]{3,2,1,0:T(8,128)(2,1)}, u32[]{:S(2)}, u32[]{:S(2)}) collective-permute-start(bf16[4,2,32,640]{3,2,1,0:T(8,128)(2,1)S(1)} %collective-permute-done.1.refs_1_), channel_id=1, source_target_pairs={{8,0},{9,1},{10,2},{11,3},{12,4},{13,5},{14,6},{15,7},{16,8},{17,9... | collective-permute-start | bytes 983048 | tf_op jit(solution)/shard_map/ppermute | solution.py:30
Sparse Core Ops, SparseCore 0:
  10.5 104.3 all-gather.1
